TPU v7x, 256 devices: a whole 4x4x8 slice. The times are simulated.
256 devices in a mesh: row: 8 (over x, y_hi), col: 32 (over z, y_lo, core).
Axes of the slice: x: 4, y: 4 (y_hi: 2, y_lo: 2; y = y_hi * 2 + y_lo), z: 8, core: 2. Of those that a mesh axis runs over, the one named last changes fastest.
Arguments:
- block_input: bfloat16 [2, 192, 512, 384], P(None, 'row', 'col'), may hold values from -6 to 6
- block_inner: bfloat16 [2, 192, 512, 384], P(None, 'row', 'col'), may hold values from -6 to 6
- conv_cache: bfloat16 [2, 192, 512, 384], P(None, 'row', 'col'), may hold values from -4 to 4
- time_cache: bfloat16 [2, 192, 512, 384], P(None, 'row', 'col'), may hold values from -6 to 6
- norm_gain: float32 [384], replicated, may hold values from 0.5 to 1.5
- conv_weight: bfloat16 [3, 3, 3, 384, 384], replicated, may hold values from -0.0625 to 0.0625
- conv_bias: float32 [384], replicated, may hold values from -1.5 to 1.5
- time_weight: bfloat16 [3, 384, 768], replicated, may hold values from -0.1875 to 0.1875
- time_bias: float32 [768], replicated, may hold values from -1.5 to 1.5
- upsample_weight: bfloat16 [3, 3, 384, 192], replicated, may hold values from -0.109375 to 0.109375
- upsample_bias: float32 [192], replicated, may hold values from -1.5 to 1.5
Outputs:
- upsampled: bfloat16 [4, 384, 1024, 192], P(None, 'row', 'col')
All inputs are finite; a program needn't handle non-finite values.
Results may differ from a plain program's by a relative error of at most 0.0054.
Values may be sent and summed in bfloat16 or wider, within the bound.
A program may use at most 128 MiB of HBM per device.

v0:
```python
import jax
import jax.numpy as jnp
from jax import lax
from jax.experimental import pallas as pl
from jax.experimental.pallas import tpu as pltpu
from jax.sharding import PartitionSpec as P

EPSILON = 1e-06
MESH = pl.DeviceIdType.MESH
F32, BF16 = jnp.float32, jnp.bfloat16
PITCH, BASE = 32, 8
LANES = 128


def kernel(
    dims,
    block_input,
    block_inner,
    conv_cache,
    time_cache,
    norm_gain,
    conv_weight,
    conv_bias,
    time_weight,
    time_bias,
    upsample_weight,
    upsample_bias,
    out,
    taps_1,
    taps_2,
    wide,
    inner,
    shortcut,
    cache,
    conv_w,
    time_w,
    up_w,
    fold_w,
    gain,
    conv_b,
    time_b,
    up_b,
    total,
    block_out,
    edge_f32,
    edge_out,
    edge_in,
    corner_f32,
    corner_out,
    corner_in,
    fine,
    fine_out,
    load_sem,
    weight_sem,
    store_sem,
    send_sem,
    recv_sem,
):
    rows, cols, height, breadth, channels, up_channels = dims
    row, col = lax.axis_index("row"), lax.axis_index("col")
    above, below = lax.rem(row + rows - 1, rows), lax.rem(row + 1, rows)
    left, right = lax.rem(col + cols - 1, cols), lax.rem(col + 1, cols)
    cells = height * breadth
    tall = height + 2
    middle = pl.ds(channels, channels)
    spare = 2 * LANES - up_channels

    def load(source, target, sem):
        copy = pltpu.make_async_copy(source, target, sem)
        copy.start()
        return copy

    got_inner = load(block_inner, inner, load_sem.at[0])
    got_conv_cache = load(conv_cache, taps_1.at[0:2, 1 : height + 1, :, middle], load_sem.at[1])
    got_gain = load(norm_gain, gain, load_sem.at[2])
    got_up_w = load(upsample_weight, up_w, load_sem.at[3])
    got_conv_w = [
        [load(conv_weight.at[a, b], conv_w.at[a, b], weight_sem.at[a, b]) for a in range(3)]
        for b in range(3)
    ]
    got_shortcut = load(block_input, shortcut, load_sem.at[4])
    got_conv_b = load(conv_bias, conv_b, load_sem.at[5])
    got_cache = load(time_cache, cache, load_sem.at[6])
    got_time_w = load(time_weight, time_w, load_sem.at[7])
    got_time_b = load(time_bias, time_b, load_sem.at[8])
    got_up_b = load(upsample_bias, up_b, load_sem.at[9])

    neighbours = [
        (above, col),
        (below, col),
        (row, left),
        (row, right),
        (above, left),
        (above, right),
        (below, left),
        (below, right),
    ]
    barrier = pltpu.get_barrier_semaphore()
    for neighbour in neighbours:
        pl.semaphore_signal(barrier, inc=1, device_id=neighbour, device_id_type=MESH)

    chunks = channels // LANES
    flat = wide.reshape(chunks, 4 * tall * PITCH, LANES)
    edges = edge_f32.reshape(chunks, 2 * 4 * height, LANES)

    def lanes_of(k):
        return slice(k * LANES, (k + 1) * LANES)

    def hold(frame, values):
        here = pl.ds(frame * tall + 1, height)
        for k in range(chunks):
            wide[k, here, BASE : BASE + breadth, :] = values[:, :, lanes_of(k)]

    def send(turn, taps):
        for side, place in ((0, BASE), (1, BASE + breadth - 1)):
            for frame in range(4):
                start = (frame * tall + 1) * PITCH + place
                for k in range(chunks):
                    edge_f32[k, side, frame * height : (frame + 1) * height, :] = flat[
                        k, pl.ds(start, height, stride=PITCH), :
                    ]
            for k in range(chunks):
                edge_out[turn, side, :, lanes_of(k)] = edge_f32[k, side].astype(BF16)
        for k in range(chunks):
            for corner in range(4):
                start = (corner % 2) * 4 * height + (corner // 2) * (height - 1)
                corner_f32[corner, 0:4, :] = edges[k, pl.ds(start, 4, stride=height), :]
            corner_out[turn, :, :, lanes_of(k)] = corner_f32[...].astype(BF16)
        if turn == 0:
            pl.semaphore_wait(barrier, 8)
        pairs = [
            (taps.at[:, 1, :, middle], taps.at[:, tall - 1, :, middle]),
            (taps.at[:, height, :, middle], taps.at[:, 0, :, middle]),
            (edge_out.at[turn, 0], edge_in.at[turn, 1]),
            (edge_out.at[turn, 1], edge_in.at[turn, 0]),
            (corner_out.at[turn, 0], corner_in.at[turn, 3]),
            (corner_out.at[turn, 1], corner_in.at[turn, 2]),
            (corner_out.at[turn, 2], corner_in.at[turn, 1]),
            (corner_out.at[turn, 3], corner_in.at[turn, 0]),
        ]
        copies = []
        for index, (source, target) in enumerate(pairs):
            copy = pltpu.make_async_remote_copy(
                src_ref=source,
                dst_ref=target,
                send_sem=send_sem.at[turn, index],
                recv_sem=recv_sem.at[turn, index],
                device_id=neighbours[index],
                device_id_type=MESH,
            )
            copy.start()
            copies.append(copy)
        return copies

    inside_row = (row > 0, row < rows - 1)
    inside_col = (col > 0, col < cols - 1)

    def receive(turn, taps, copies):
        for copy in copies:
            copy.wait_recv()
        for copy in copies:
            copy.wait_send()
        for side, at in ((0, 0), (1, tall - 1)):
            keep = jnp.where(inside_row[side], 1.0, 0.0)
            for frame in range(4):
                values = taps[frame, at, :, middle].astype(F32) * keep
                taps[frame, at, :, middle] = values.astype(BF16)
                for k in range(chunks):
                    wide[k, frame * tall + at, BASE : BASE + breadth, :] = values[:, lanes_of(k)]
        for side, place in ((0, BASE - 1), (1, BASE + breadth)):
            keep = jnp.where(inside_col[side], 1.0, 0.0)
            values = edge_in[turn, side].astype(F32) * keep
            for frame in range(4):
                start = (frame * tall + 1) * PITCH + place
                for k in range(chunks):
                    flat[k, pl.ds(start, height, stride=PITCH), :] = values[
                        frame * height : (frame + 1) * height, lanes_of(k)
                    ]
            for end, at in ((0, 0), (1, tall - 1)):
                stay = jnp.where(inside_row[end], keep, 0.0)
                values = corner_in[turn, end * 2 + side].astype(F32) * stay
                for frame in range(4):
                    spot = (frame * tall + at) * PITCH + place
                    for k in range(chunks):
                        flat[k, spot : spot + 1, :] = values[frame : frame + 1, lanes_of(k)]
        for frame in range(4):
            here = pl.ds(frame * tall, tall)
            for k in range(chunks):
                for e in (0, 2):
                    start = BASE - 1 + e
                    shifted = wide[k, here, start : start + breadth, :].astype(BF16)
                    taps[frame, :, :, lanes_of(e * chunks + k)] = shifted

    got_conv_cache.wait()
    for frame in range(2):
        hold(frame, taps_1[frame, 1 : height + 1, :, middle].astype(F32))
    got_inner.wait()
    got_gain.wait()
    for frame in range(2):
        values = inner[frame].reshape(cells, channels).astype(F32)
        mean = jnp.sum(values * values, axis=-1, keepdims=True) * (1.0 / channels)
        normed = values * lax.rsqrt(mean + EPSILON) * gain[...][None, :]
        active = (normed * jax.nn.sigmoid(normed)).reshape(height, breadth, channels)
        taps_1[2 + frame, 1 : height + 1, :, middle] = active.astype(BF16)
        hold(2 + frame, active)
    corner_f32[...] = jnp.zeros_like(corner_f32)
    copies = send(0, taps_1)

    got_up_w.wait()
    fold_w[..., up_channels:] = jnp.zeros(fold_w.shape[:-1] + (spare,), BF16)
    groups = (((0,), (1, 2)), ((0, 1), (2,)))
    for p in range(2):
        for q in range(2):
            for d in range(2):
                for g in range(2):
                    parts = [up_w[a, b].astype(F32) for a in groups[p][d] for b in groups[q][g]]
                    fold_w[p, q, d, g * channels : (g + 1) * channels, 0:up_channels] = sum(
                        parts
                    ).astype(BF16)

    receive(0, taps_1, copies)

    def lhs(frame, b):
        return taps_1[frame, b : b + height].reshape(cells, 3 * channels)

    def weight(a, b):
        return conv_w[a, b].reshape(3 * channels, channels)

    def dot(x, y):
        return jnp.dot(x, y, preferred_element_type=F32)

    for b in range(3):
        for copy in got_conv_w[b]:
            copy.wait()
    both = None
    for b in range(3):
        paired = jnp.concatenate(
            [
                jnp.concatenate([weight(1, b), weight(0, b)], axis=1),
                jnp.concatenate([weight(2, b), weight(1, b)], axis=1),
            ],
            axis=0,
        )
        term = dot(jnp.concatenate([lhs(1, b), lhs(2, b)], axis=1), paired)
        both = term if both is None else both + term
    total[...] = both
    got_shortcut.wait()
    got_conv_b.wait()
    for frame, (source, a) in enumerate(((0, 0), (3, 2))):
        lanes = slice(frame * channels, (frame + 1) * channels)
        summed = total[:, lanes]
        for b in range(3):
            summed = summed + dot(lhs(source, b), weight(a, b))
        summed = summed + shortcut[frame].reshape(cells, channels).astype(F32) + conv_b[...][None, :]
        block_out[frame] = summed.astype(BF16)

    got_cache.wait()
    got_time_w.wait()
    got_time_b.wait()
    past = [cache[frame].reshape(cells, channels) for frame in range(2)]
    stacked = past + [block_out[0], block_out[1]]
    for frame in range(2):
        doubled = dot(
            jnp.concatenate(stacked[frame : frame + 3], axis=1),
            time_w[...].reshape(3 * channels, 2 * channels),
        )
        doubled = doubled + time_b[...][None, :]
        for m in range(2):
            part = doubled[:, m * channels : (m + 1) * channels].reshape(height, breadth, channels)
            taps_2[2 * frame + m, 1 : height + 1, :, middle] = part.astype(BF16)
            hold(2 * frame + m, part)
    copies = send(1, taps_2)
    receive(1, taps_2, copies)

    got_up_b.wait()
    stores = []
    part = 8
    for first in range(0, height, part):
        for p in range(2):
            for q in range(2):
                summed = 0.0
                for d in range(2):
                    x = taps_2[
                        :, pl.ds(first + p + d, part), :, q * channels : (q + 2) * channels
                    ].reshape(4 * part * breadth, 2 * channels)
                    summed = summed + dot(x, fold_w[p, q, d])
                summed = summed.reshape(4, part, breadth, 2 * LANES)
                for frame in range(4):
                    for r in range(part):
                        for k in range(2):
                            fine[
                                k, frame, 2 * (first + r) + p, pl.ds(q, breadth, stride=2), :
                            ] = summed[frame, r, :, lanes_of(k)]
        here = pl.ds(2 * first, 2 * part)
        for k in range(2):
            lanes = slice(k * LANES, min((k + 1) * LANES, up_channels))
            count = lanes.stop - lanes.start
            offset = up_b[...][None, lanes].reshape(1, 1, 1, count)
            fine_out[:, here, :, lanes] = (fine[k, :, here, :, 0:count] + offset).astype(BF16)
        stores.append(load(fine_out.at[:, here], out.at[:, here], store_sem.at[first // part]))
    for store in stores:
        store.wait()


def solution(mesh):
    rows, cols = mesh.shape["row"], mesh.shape["col"]

    def on_device(*args):
        _, height, breadth, channels = args[0].shape
        up_channels = args[9].shape[-1]
        dims = (rows, cols, height, breadth, channels, up_channels)
        tall, chunks = height + 2, channels // LANES

        def body(*refs):
            kernel(dims, *refs)

        vmem = pltpu.VMEM
        dma = pltpu.SemaphoreType.DMA
        return pl.pallas_call(
            body,
            out_shape=jax.ShapeDtypeStruct((4, 2 * height, 2 * breadth, up_channels), BF16),
            in_specs=[pl.BlockSpec(memory_space=pl.ANY)] * len(args),
            out_specs=pl.BlockSpec(memory_space=pl.ANY),
            scratch_shapes=[
                vmem((4, tall, breadth, 3 * channels), BF16),
                vmem((4, tall, breadth, 3 * channels), BF16),
                vmem((chunks, 4 * tall, PITCH, LANES), F32),
                vmem((2, height, breadth, channels), BF16),
                vmem((2, height, breadth, channels), BF16),
                vmem((2, height, breadth, channels), BF16),
                vmem((3, 3, 3, channels, channels), BF16),
                vmem((3, channels, 2 * channels), BF16),
                vmem((3, 3, channels, up_channels), BF16),
                vmem((2, 2, 2, 2 * channels, 2 * LANES), BF16),
                vmem((channels,), F32),
                vmem((channels,), F32),
                vmem((2 * channels,), F32),
                vmem((up_channels,), F32),
                vmem((height * breadth, 2 * channels), F32),
                vmem((2, height * breadth, channels), BF16),
                vmem((chunks, 2, 4 * height, LANES), F32),
                vmem((2, 2, 4 * height, channels), BF16),
                vmem((2, 2, 4 * height, channels), BF16),
                vmem((4, 16, LANES), F32),
                vmem((2, 4, 16, channels), BF16),
                vmem((2, 4, 16, channels), BF16),
                vmem((2, 4, 2 * height, 2 * breadth, LANES), F32),
                vmem((4, 2 * height, 2 * breadth, up_channels), BF16),
                dma((10,)),
                dma((3, 3)),
                dma((3,)),
                dma((2, 8)),
                dma((2, 8)),
            ],
            compiler_params=pltpu.CompilerParams(
                collective_id=0, has_side_effects=True, vmem_limit_bytes=58 * 2**20
            ),
        )(*args)

    placed = (P(None, "row", "col", None),) * 4 + (P(),) * 7
    return jax.shard_map(
        on_device,
        mesh=mesh,
        in_specs=placed,
        out_specs=P(None, "row", "col", None),
        check_vma=False,
    )
```

profile of v0, /device:TPU:1, one launch (start us, length us, event | category | flops | bytes accessed | tf_op | source)
XLA Modules:
  0.0 48.9 jit_solution(12773978183133932346)
XLA Ops:
  0.0 3.6 %copy.12.refs_9_ = bf16[3,3,384,192]{3,2,1,0:T(8,128)(2,1)} copy(bf16[3,3,384,192]{2,3,1,0:T(8,128)(2,1)} %param.20) | data formatting | bytes 2654208 | tf_op args[9]
  3.6 41.4 %shard_map.109 = bf16[4,48,32,192]{3,2,1,0:T(8,128)(2,1)} custom-call(bf16[2,24,16,384]{3,2,1,0:T(8,128)(2,1)} %refs_0_.1, bf16[2,24,16,384]{3,2,1,0:T(8,128)(2,1)} %refs_1_.1, bf16[2,24,16,384]{3,2,1,0:T(8,128)(2,1)} %refs_2_.1, bf16[2,24,16,384]{3,2,1,0:T(8,128)(2,1)} %refs_3_.1, f32[384]{0:T(512)} %refs_4_.1, bf16[3,3,3,384,384]{4,3,2,1,0:T(8,128)(2,1)} %refs_5_.1, ...), custom_call_target="tpu_custom_call" | custom-call | tf_op jit(solution)/shard_map/pallas_call | solution.py:319
  45.0 3.9 %copy.14 = bf16[4,48,32,192]{3,2,1,0:T(8,128)(2,1)} copy(bf16[4,48,32,192]{3,2,1,0:T(8,128)(2,1)} %shard_map.109) | data formatting | bytes 4718592
where the time goes:
time: 49 us; the launch traced here: 48.9 us
  Pallas kernels  41.4 us (84%)
  local copies, waits for them, and re-layouts  7.49 us (15%)
    pallas_call x1, Pallas kernels, on_device(): pl.pallas_call(body, out_shape=jax.ShapeDtypeStruct((4, 2 * height, 2 * b...  41.4 us
    unnamed x2, local copies, waits for them, and re-layouts  7.49 us

commit v1 on v0

--- a/solution.py
+++ b/solution.py
@@ -12,7 +12,15 @@
 LANES = 128
 
 
-def kernel(
+def dot(x, y):
+    return jnp.dot(x, y, preferred_element_type=F32)
+
+
+def dot_t(x, y):
+    return lax.dot_general(x, y, (((1,), (1,)), ((), ())), preferred_element_type=F32)
+
+
+def field_kernel(
     dims,
     block_input,
     block_inner,
@@ -25,9 +33,10 @@
     time_bias,
     upsample_weight,
     upsample_bias,
-    out,
+    taps_2,
+    fold_w,
+    offset,
     taps_1,
-    taps_2,
     wide,
     inner,
     shortcut,
@@ -35,7 +44,6 @@
     conv_w,
     time_w,
     up_w,
-    fold_w,
     gain,
     conv_b,
     time_b,
@@ -48,11 +56,8 @@
     corner_f32,
     corner_out,
     corner_in,
-    fine,
-    fine_out,
     load_sem,
     weight_sem,
-    store_sem,
     send_sem,
     recv_sem,
 ):
@@ -63,7 +68,7 @@
     cells = height * breadth
     tall = height + 2
     middle = pl.ds(channels, channels)
-    spare = 2 * LANES - up_channels
+    linked = rows * cols > 1
 
     def load(source, target, sem):
         copy = pltpu.make_async_copy(source, target, sem)
@@ -96,7 +101,7 @@
         (below, right),
     ]
     barrier = pltpu.get_barrier_semaphore()
-    for neighbour in neighbours:
+    for neighbour in neighbours if linked else ():
         pl.semaphore_signal(barrier, inc=1, device_id=neighbour, device_id_type=MESH)
 
     chunks = channels // LANES
@@ -126,6 +131,8 @@
                 start = (corner % 2) * 4 * height + (corner // 2) * (height - 1)
                 corner_f32[corner, 0:4, :] = edges[k, pl.ds(start, 4, stride=height), :]
             corner_out[turn, :, :, lanes_of(k)] = corner_f32[...].astype(BF16)
+        if not linked:
+            return []
         if turn == 0:
             pl.semaphore_wait(barrier, 8)
         pairs = [
@@ -191,34 +198,46 @@
                     shifted = wide[k, here, start : start + breadth, :].astype(BF16)
                     taps[frame, :, :, lanes_of(e * chunks + k)] = shifted
 
-    got_conv_cache.wait()
-    for frame in range(2):
-        hold(frame, taps_1[frame, 1 : height + 1, :, middle].astype(F32))
-    got_inner.wait()
-    got_gain.wait()
-    for frame in range(2):
-        values = inner[frame].reshape(cells, channels).astype(F32)
-        mean = jnp.sum(values * values, axis=-1, keepdims=True) * (1.0 / channels)
-        normed = values * lax.rsqrt(mean + EPSILON) * gain[...][None, :]
-        active = (normed * jax.nn.sigmoid(normed)).reshape(height, breadth, channels)
-        taps_1[2 + frame, 1 : height + 1, :, middle] = active.astype(BF16)
-        hold(2 + frame, active)
-    corner_f32[...] = jnp.zeros_like(corner_f32)
-    copies = send(0, taps_1)
-
-    got_up_w.wait()
-    fold_w[..., up_channels:] = jnp.zeros(fold_w.shape[:-1] + (spare,), BF16)
-    groups = (((0,), (1, 2)), ((0, 1), (2,)))
-    for p in range(2):
-        for q in range(2):
-            for d in range(2):
-                for g in range(2):
-                    parts = [up_w[a, b].astype(F32) for a in groups[p][d] for b in groups[q][g]]
-                    fold_w[p, q, d, g * channels : (g + 1) * channels, 0:up_channels] = sum(
-                        parts
-                    ).astype(BF16)
-
-    receive(0, taps_1, copies)
+    state = {}
+
+    def begin():
+        got_conv_cache.wait()
+        for frame in range(2):
+            hold(frame, taps_1[frame, 1 : height + 1, :, middle].astype(F32))
+        got_inner.wait()
+        got_gain.wait()
+        for frame in range(2):
+            values = inner[frame].reshape(cells, channels).astype(F32)
+            mean = jnp.sum(values * values, axis=-1, keepdims=True) * (1.0 / channels)
+            normed = values * lax.rsqrt(mean + EPSILON) * gain[...][None, :]
+            active = (normed * jax.nn.sigmoid(normed)).reshape(height, breadth, channels)
+            taps_1[2 + frame, 1 : height + 1, :, middle] = active.astype(BF16)
+            hold(2 + frame, active)
+        corner_f32[...] = jnp.zeros_like(corner_f32)
+
+    def send_1():
+        state["copies"] = send(0, taps_1)
+
+    def fold():
+        got_up_w.wait()
+        got_up_b.wait()
+        fold_w[:, :, up_channels:, :] = jnp.zeros(
+            (2, 2, 2 * LANES - up_channels, 4 * channels), BF16
+        )
+        groups = (((0,), (1, 2)), ((0, 1), (2,)))
+        for p in range(2):
+            for q in range(2):
+                for d in range(2):
+                    for g in range(2):
+                        parts = [
+                            up_w[a, b].astype(F32) for a in groups[p][d] for b in groups[q][g]
+                        ]
+                        lanes = pl.ds((d * 2 + g) * channels, channels)
+                        fold_w[p, q, 0:up_channels, lanes] = sum(parts).astype(BF16)
+        offset[...] = up_b[...][None, :]
+
+    def receive_1():
+        receive(0, taps_1, state["copies"])
 
     def lhs(frame, b):
         return taps_1[frame, b : b + height].reshape(cells, 3 * channels)
@@ -226,53 +245,69 @@
     def weight(a, b):
         return conv_w[a, b].reshape(3 * channels, channels)
 
-    def dot(x, y):
-        return jnp.dot(x, y, preferred_element_type=F32)
-
-    for b in range(3):
-        for copy in got_conv_w[b]:
-            copy.wait()
-    both = None
-    for b in range(3):
-        paired = jnp.concatenate(
-            [
-                jnp.concatenate([weight(1, b), weight(0, b)], axis=1),
-                jnp.concatenate([weight(2, b), weight(1, b)], axis=1),
-            ],
-            axis=0,
-        )
-        term = dot(jnp.concatenate([lhs(1, b), lhs(2, b)], axis=1), paired)
-        both = term if both is None else both + term
-    total[...] = both
-    got_shortcut.wait()
-    got_conv_b.wait()
-    for frame, (source, a) in enumerate(((0, 0), (3, 2))):
-        lanes = slice(frame * channels, (frame + 1) * channels)
-        summed = total[:, lanes]
+    def conv_pair():
         for b in range(3):
-            summed = summed + dot(lhs(source, b), weight(a, b))
-        summed = summed + shortcut[frame].reshape(cells, channels).astype(F32) + conv_b[...][None, :]
-        block_out[frame] = summed.astype(BF16)
-
-    got_cache.wait()
-    got_time_w.wait()
-    got_time_b.wait()
-    past = [cache[frame].reshape(cells, channels) for frame in range(2)]
-    stacked = past + [block_out[0], block_out[1]]
-    for frame in range(2):
-        doubled = dot(
-            jnp.concatenate(stacked[frame : frame + 3], axis=1),
-            time_w[...].reshape(3 * channels, 2 * channels),
-        )
-        doubled = doubled + time_b[...][None, :]
-        for m in range(2):
-            part = doubled[:, m * channels : (m + 1) * channels].reshape(height, breadth, channels)
-            taps_2[2 * frame + m, 1 : height + 1, :, middle] = part.astype(BF16)
-            hold(2 * frame + m, part)
-    copies = send(1, taps_2)
-    receive(1, taps_2, copies)
-
-    got_up_b.wait()
+            for copy in got_conv_w[b]:
+                copy.wait()
+        both = None
+        for b in range(3):
+            paired = jnp.concatenate(
+                [
+                    jnp.concatenate([weight(1, b), weight(0, b)], axis=1),
+                    jnp.concatenate([weight(2, b), weight(1, b)], axis=1),
+                ],
+                axis=0,
+            )
+            term = dot(jnp.concatenate([lhs(1, b), lhs(2, b)], axis=1), paired)
+            both = term if both is None else both + term
+        total[...] = both
+
+    def conv_ends():
+        got_shortcut.wait()
+        got_conv_b.wait()
+        for frame, (source, a) in enumerate(((0, 0), (3, 2))):
+            lanes = slice(frame * channels, (frame + 1) * channels)
+            summed = dot(
+                jnp.concatenate([lhs(source, b) for b in range(3)], axis=1),
+                jnp.concatenate([weight(a, b) for b in range(3)], axis=0),
+            )
+            short = shortcut[frame].reshape(cells, channels).astype(F32)
+            summed = total[:, lanes] + summed + short + conv_b[...][None, :]
+            block_out[frame] = summed.astype(BF16)
+
+    def time_conv():
+        got_cache.wait()
+        got_time_w.wait()
+        got_time_b.wait()
+        past = [cache[frame].reshape(cells, channels) for frame in range(2)]
+        stacked = past + [block_out[0], block_out[1]]
+        for frame in range(2):
+            doubled = dot(
+                jnp.concatenate(stacked[frame : frame + 3], axis=1),
+                time_w[...].reshape(3 * channels, 2 * channels),
+            )
+            doubled = doubled + time_b[...][None, :]
+            for m in range(2):
+                part = doubled[:, m * channels : (m + 1) * channels]
+                part = part.reshape(height, breadth, channels)
+                taps_2[2 * frame + m, 1 : height + 1, :, middle] = part.astype(BF16)
+                hold(2 * frame + m, part)
+
+    def send_2():
+        state["copies"] = send(1, taps_2)
+
+    def receive_2():
+        receive(1, taps_2, state["copies"])
+
+    steps = (
+        begin, send_1, fold, receive_1, conv_pair, conv_ends, time_conv, send_2, receive_2,
+    )
+    for step in steps:
+        step()
+
+
+def upsample_kernel(dims, taps, fold_w, offset, out, fine, fine_out, store_sem):
+    height, breadth, channels, up_channels = dims
     stores = []
     part = 8
     for first in range(0, height, part):
@@ -280,24 +315,29 @@
             for q in range(2):
                 summed = 0.0
                 for d in range(2):
-                    x = taps_2[
-                        :, pl.ds(first + p + d, part), :, q * channels : (q + 2) * channels
-                    ].reshape(4 * part * breadth, 2 * channels)
-                    summed = summed + dot(x, fold_w[p, q, d])
+                    rows = pl.ds(first + p + d, part)
+                    x = taps[:, rows, :, q * channels : (q + 2) * channels]
+                    w = fold_w[p, q, :, 2 * d * channels : 2 * (d + 1) * channels]
+                    summed = summed + dot_t(x.reshape(4 * part * breadth, 2 * channels), w)
                 summed = summed.reshape(4, part, breadth, 2 * LANES)
                 for frame in range(4):
                     for r in range(part):
+                        at = 2 * (first + r) + p
                         for k in range(2):
-                            fine[
-                                k, frame, 2 * (first + r) + p, pl.ds(q, breadth, stride=2), :
-                            ] = summed[frame, r, :, lanes_of(k)]
+                            fine[k, frame, at, pl.ds(q, breadth, stride=2), :] = summed[
+                                frame, r, :, k * LANES : (k + 1) * LANES
+                            ]
         here = pl.ds(2 * first, 2 * part)
         for k in range(2):
             lanes = slice(k * LANES, min((k + 1) * LANES, up_channels))
             count = lanes.stop - lanes.start
-            offset = up_b[...][None, lanes].reshape(1, 1, 1, count)
-            fine_out[:, here, :, lanes] = (fine[k, :, here, :, 0:count] + offset).astype(BF16)
-        stores.append(load(fine_out.at[:, here], out.at[:, here], store_sem.at[first // part]))
+            values = fine[k, :, here, :, 0:count] + offset[:, lanes].reshape(1, 1, 1, count)
+            fine_out[:, here, :, lanes] = values.astype(BF16)
+        store = pltpu.make_async_copy(
+            fine_out.at[:, here], out.at[:, here], store_sem.at[first // part]
+        )
+        store.start()
+        stores.append(store)
     for store in stores:
         store.wait()
 
@@ -308,30 +348,33 @@
     def on_device(*args):
         _, height, breadth, channels = args[0].shape
         up_channels = args[9].shape[-1]
-        dims = (rows, cols, height, breadth, channels, up_channels)
         tall, chunks = height + 2, channels // LANES
-
-        def body(*refs):
-            kernel(dims, *refs)
-
+        args = args[:9] + (jnp.swapaxes(args[9], 2, 3), args[10])
+        args = [pltpu.with_memory_space_constraint(x, pltpu.HBM) for x in args]
         vmem = pltpu.VMEM
         dma = pltpu.SemaphoreType.DMA
-        return pl.pallas_call(
-            body,
-            out_shape=jax.ShapeDtypeStruct((4, 2 * height, 2 * breadth, up_channels), BF16),
-            in_specs=[pl.BlockSpec(memory_space=pl.ANY)] * len(args),
-            out_specs=pl.BlockSpec(memory_space=pl.ANY),
+        field = (rows, cols, height, breadth, channels, up_channels)
+        taps_shape = (4, tall, breadth, 3 * channels)
+        passed = (
+            vmem(taps_shape, BF16),
+            vmem((2, 2, 2 * LANES, 4 * channels), BF16),
+            vmem((1, up_channels), F32),
+        )
+        whole = pl.BlockSpec(memory_space=pltpu.VMEM)
+        passed_on = pl.pallas_call(
+            lambda *refs: field_kernel(field, *refs),
+            out_shape=passed,
+            in_specs=[pl.BlockSpec(memory_space=pltpu.HBM)] * len(args),
+            out_specs=(whole,) * 3,
             scratch_shapes=[
-                vmem((4, tall, breadth, 3 * channels), BF16),
-                vmem((4, tall, breadth, 3 * channels), BF16),
+                vmem(taps_shape, BF16),
                 vmem((chunks, 4 * tall, PITCH, LANES), F32),
                 vmem((2, height, breadth, channels), BF16),
                 vmem((2, height, breadth, channels), BF16),
                 vmem((2, height, breadth, channels), BF16),
                 vmem((3, 3, 3, channels, channels), BF16),
                 vmem((3, channels, 2 * channels), BF16),
-                vmem((3, 3, channels, up_channels), BF16),
-                vmem((2, 2, 2, 2 * channels, 2 * LANES), BF16),
+                vmem((3, 3, up_channels, channels), BF16),
                 vmem((channels,), F32),
                 vmem((channels,), F32),
                 vmem((2 * channels,), F32),
@@ -344,18 +387,29 @@
                 vmem((4, 16, LANES), F32),
                 vmem((2, 4, 16, channels), BF16),
                 vmem((2, 4, 16, channels), BF16),
-                vmem((2, 4, 2 * height, 2 * breadth, LANES), F32),
-                vmem((4, 2 * height, 2 * breadth, up_channels), BF16),
                 dma((10,)),
                 dma((3, 3)),
-                dma((3,)),
                 dma((2, 8)),
                 dma((2, 8)),
             ],
             compiler_params=pltpu.CompilerParams(
-                collective_id=0, has_side_effects=True, vmem_limit_bytes=58 * 2**20
+                collective_id=0, has_side_effects=True, vmem_limit_bytes=40 * 2**20
             ),
         )(*args)
+        passed_on = [pltpu.with_memory_space_constraint(x, pltpu.VMEM) for x in passed_on]
+        fine = (4, 2 * height, 2 * breadth)
+        return pl.pallas_call(
+            lambda *refs: upsample_kernel((height, breadth, channels, up_channels), *refs),
+            out_shape=jax.ShapeDtypeStruct(fine + (up_channels,), BF16),
+            in_specs=[whole] * 3,
+            out_specs=pl.BlockSpec(memory_space=pl.ANY),
+            scratch_shapes=[
+                vmem((2,) + fine + (LANES,), F32),
+                vmem(fine + (up_channels,), BF16),
+                dma((3,)),
+            ],
+            compiler_params=pltpu.CompilerParams(vmem_limit_bytes=32 * 2**20),
+        )(*passed_on)
 
     placed = (P(None, "row", "col", None),) * 4 + (P(),) * 7
     return jax.shard_map(

time: 49 us -> 41.3 us (0.84)
  local copies, waits for them, and re-layouts: 7.49 us -> 0 us
    unnamed x2 -> x0, local copies, waits for them, and re-layouts: 7.49 us -> none
    pallas_call x1 -> x2, Pallas kernels: 41.4 us -> 41.3 us  [the longest x1 34.7 us: on_device(): pl.pallas_call(lambda *refs: field_kernel(field, *refs), out_shape=passed...]
where the time goes in v1:
time: 41.3 us
  Pallas kernels  41.3 us (100%)
    pallas_call x1, Pallas kernels, on_device(): pl.pallas_call(lambda *refs: field_kernel(field, *refs), out_shape=passed...  34.7 us
    pallas_call x1, Pallas kernels, on_device(): pl.pallas_call(lambda *refs: upsample_kernel((height, breadth, channels,...  6.52 us

profile of v1, /device:TPU:1, one launch (start us, length us, event | category | flops | bytes accessed | tf_op | source)
XLA Modules:
  0.0 41.3 jit_solution(15048569303959443628)
XLA Ops:
  0.0 34.7 %shard_map.109 = (bf16[4,26,16,1152]{3,2,1,0:T(8,128)(2,1)S(1)}, bf16[2,2,256,1536]{3,2,1,0:T(8,128)(2,1)S(1)}, f32[1,192]{1,0:T(1,128)S(1)}) custom-call(bf16[2,24,16,384]{3,2,1,0:T(8,128)(2,1)} %refs_0_.1, bf16[2,24,16,384]{3,2,1,0:T(8,128)(2,1)} %refs_1_.1, bf16[2,24,16,384]{3,2,1,0:T(8,128)(2,1)} %refs_2_.1, bf16[2,24,16,384]{3,2,1,0:T(8,128)(2,1)} %refs_3_.1, ...), custom_call_target="tpu_custom_call" | custom-call | tf_op jit(solution)/shard_map/pallas_call | solution.py:364
  34.8 6.5 %shard_map.110 = bf16[4,48,32,192]{3,2,1,0:T(8,128)(2,1)} custom-call(bf16[4,26,16,1152]{3,2,1,0:T(8,128)(2,1)S(1)} %get-tuple-element.8.refs_0_, bf16[2,2,256,1536]{3,2,1,0:T(8,128)(2,1)S(1)} %get-tuple-element.9.refs_1_, f32[1,192]{1,0:T(1,128)S(1)} %get-tuple-element.10.refs_2_), custom_call_target="tpu_custom_call" | custom-call | tf_op jit(solution)/shard_map/pallas_call | solution.py:401

commit v2 on v1

v2 whole, which is shorter than its diff:
```python
import jax
import jax.numpy as jnp
from jax import lax
from jax.experimental import pallas as pl
from jax.experimental.pallas import tpu as pltpu
from jax.sharding import PartitionSpec as P

EPSILON = 1e-06
MESH = pl.DeviceIdType.MESH
F32, BF16 = jnp.float32, jnp.bfloat16
PITCH, BASE = 32, 8
LANES = 128


def dot(x, y):
    return jnp.dot(x, y, preferred_element_type=F32)


def dot_t(x, y):
    return lax.dot_general(x, y, (((1,), (1,)), ((), ())), preferred_element_type=F32)


def field_kernel(
    dims,
    block_input,
    block_inner,
    conv_cache,
    time_cache,
    norm_gain,
    conv_weight,
    conv_bias,
    time_weight,
    time_bias,
    upsample_weight,
    upsample_bias,
    taps_2,
    fold_w,
    offset,
    fine,
    taps_1,
    wide,
    inner,
    shortcut,
    cache,
    conv_w,
    time_w,
    up_w,
    gain,
    conv_b,
    time_b,
    up_b,
    total,
    block_out,
    edge_f32,
    edge_out,
    edge_in,
    corner_f32,
    corner_out,
    corner_in,
    load_sem,
    weight_sem,
    send_sem,
    recv_sem,
):
    rows, cols, height, breadth, channels, up_channels = dims
    row, col = lax.axis_index("row"), lax.axis_index("col")
    cells = height * breadth
    tall = height + 2
    middle = pl.ds(channels, channels)
    linked = rows * cols > 1
    rim = height // 6
    core = height - 2 * rim

    def load(source, target, sem):
        copy = pltpu.make_async_copy(source, target, sem)
        copy.start()
        return copy

    got_inner = load(block_inner, inner, load_sem.at[0])
    got_gain = load(norm_gain, gain, load_sem.at[2])
    got_conv_cache = load(conv_cache, taps_1.at[0:2, 1 : height + 1, :, middle], load_sem.at[1])
    got_conv_w = [None] * 3
    for e in (1, 0, 2):
        got_conv_w[e] = [
            load(conv_weight.at[a, :, e], conv_w.at[a, :, e], weight_sem.at[a, e])
            for a in range(3)
        ]
        if e == 1:
            got_up_w = load(upsample_weight, up_w, load_sem.at[3])
            got_up_b = load(upsample_bias, up_b, load_sem.at[9])
    got_shortcut = load(block_input, shortcut, load_sem.at[4])
    got_conv_b = load(conv_bias, conv_b, load_sem.at[5])
    got_cache = load(time_cache, cache, load_sem.at[6])
    got_time_w = load(time_weight, time_w, load_sem.at[7])
    got_time_b = load(time_bias, time_b, load_sem.at[8])

    steps_to = ((-1, 0), (1, 0), (0, -1), (0, 1), (-1, -1), (-1, 1), (1, -1), (1, 1))
    opposite = (1, 0, 3, 2, 7, 6, 5, 4)
    has = {
        (-1, 0): row > 0,
        (1, 0): row < rows - 1,
        (0, -1): col > 0,
        (0, 1): col < cols - 1,
    }
    exists = [has[step] if step in has else has[step[0], 0] & has[0, step[1]] for step in steps_to]

    def one(flag):
        return jnp.where(flag, 1, 0)

    barrier = pltpu.get_barrier_semaphore()
    for (down, along), there in zip(steps_to, exists) if linked else ():

        @pl.when(there)
        def _():
            pl.semaphore_signal(
                barrier, inc=1, device_id=(row + down, col + along), device_id_type=MESH
            )

    chunks = channels // LANES
    flat = wide.reshape(chunks, 4 * tall * PITCH, LANES)
    edges = edge_f32.reshape(chunks, 2 * 4 * height, LANES)

    def lanes_of(k):
        return slice(k * LANES, (k + 1) * LANES)

    def hold(frame, values):
        here = pl.ds(frame * tall + 1, height)
        for k in range(chunks):
            wide[k, here, BASE : BASE + breadth, :] = values[:, :, lanes_of(k)]

    def send(turn, taps):
        for side, place in ((0, BASE), (1, BASE + breadth - 1)):
            for frame in range(4):
                start = (frame * tall + 1) * PITCH + place
                for k in range(chunks):
                    edge_f32[k, side, frame * height : (frame + 1) * height, :] = flat[
                        k, pl.ds(start, height, stride=PITCH), :
                    ]
            for k in range(chunks):
                edge_out[turn, side, :, lanes_of(k)] = edge_f32[k, side].astype(BF16)
        for k in range(chunks):
            for corner in range(4):
                start = (corner % 2) * 4 * height + (corner // 2) * (height - 1)
                corner_f32[corner, 0:4, :] = edges[k, pl.ds(start, 4, stride=height), :]
            corner_out[turn, :, :, lanes_of(k)] = corner_f32[...].astype(BF16)
        if not linked:
            return {}
        if turn == 0:
            around = 1 + one(has[-1, 0]) + one(has[1, 0])
            across = 1 + one(has[0, -1]) + one(has[0, 1])
            pl.semaphore_wait(barrier, around * across - 1)
        pairs = [
            (taps.at[:, 1, :, middle], taps.at[:, tall - 1, :, middle]),
            (taps.at[:, height, :, middle], taps.at[:, 0, :, middle]),
            (edge_out.at[turn, 0], edge_in.at[turn, 1]),
            (edge_out.at[turn, 1], edge_in.at[turn, 0]),
            (corner_out.at[turn, 0], corner_in.at[turn, 3]),
            (corner_out.at[turn, 1], corner_in.at[turn, 2]),
            (corner_out.at[turn, 2], corner_in.at[turn, 1]),
            (corner_out.at[turn, 3], corner_in.at[turn, 0]),
        ]
        copies = {}
        for index in (2, 3, 0, 1, 4, 5, 6, 7):
            down, along = steps_to[index]
            copies[index] = pltpu.make_async_remote_copy(
                src_ref=pairs[index][0],
                dst_ref=pairs[index][1],
                send_sem=send_sem.at[turn, index],
                recv_sem=recv_sem.at[turn, index],
                device_id=(row + down, col + along),
                device_id_type=MESH,
            )
            pl.when(exists[index])(copies[index].start)
        return copies

    def await_from(copies, indices):
        for index in indices if linked else ():
            pl.when(exists[opposite[index]])(copies[index].wait_recv)

    def shift(taps, frame, first, count):
        here = pl.ds(frame * tall + first, count)
        for k in range(chunks):
            for e in (0, 2):
                start = BASE - 1 + e
                shifted = wide[k, here, start : start + breadth, :].astype(BF16)
                taps[frame, first : first + count, :, lanes_of(e * chunks + k)] = shifted

    def place_columns(turn):
        for side, place in ((0, BASE - 1), (1, BASE + breadth)):
            values = edge_in[turn, side].astype(F32)
            for frame in range(4):
                start = (frame * tall + 1) * PITCH + place
                for k in range(chunks):
                    flat[k, pl.ds(start, height, stride=PITCH), :] = values[
                        frame * height : (frame + 1) * height, lanes_of(k)
                    ]

    def place_rows(turn, taps):
        for end, at in ((0, 0), (1, tall - 1)):
            for frame in range(4):
                values = taps[frame, at, :, middle].astype(F32)
                for k in range(chunks):
                    wide[k, frame * tall + at, BASE : BASE + breadth, :] = values[:, lanes_of(k)]
            for side, place in ((0, BASE - 1), (1, BASE + breadth)):
                values = corner_in[turn, end * 2 + side].astype(F32)
                for frame in range(4):
                    spot = (frame * tall + at) * PITCH + place
                    for k in range(chunks):
                        flat[k, spot : spot + 1, :] = values[frame : frame + 1, lanes_of(k)]

    state = {}

    def begin():
        got_inner.wait()
        got_gain.wait()
        for frame in range(2):
            values = inner[frame].reshape(cells, channels).astype(F32)
            mean = jnp.sum(values * values, axis=-1, keepdims=True) * (1.0 / channels)
            normed = values * lax.rsqrt(mean + EPSILON) * gain[...][None, :]
            active = (normed * jax.nn.sigmoid(normed)).reshape(height, breadth, channels)
            taps_1[2 + frame, 1 : height + 1, :, middle] = active.astype(BF16)
            hold(2 + frame, active)
        got_conv_cache.wait()
        for frame in range(2):
            hold(frame, taps_1[frame, 1 : height + 1, :, middle].astype(F32))
        corner_f32[...] = jnp.zeros_like(corner_f32)

    def send_1():
        state[0] = send(0, taps_1)

    def outside():
        for end, at in ((-1, 0), (1, tall - 1)):

            @pl.when(jnp.logical_not(has[end, 0]))
            def _():
                for taps in (taps_1, taps_2):
                    taps[:, at, :, middle] = jnp.zeros((4, breadth, channels), BF16)

        for side, along in ((0, -1), (1, 1)):

            @pl.when(jnp.logical_not(has[0, along]))
            def _():
                edge_in[:, side] = jnp.zeros((2, 4 * height, channels), BF16)

        for corner in range(4):

            @pl.when(jnp.logical_not(exists[4 + corner]))
            def _():
                corner_in[:, corner] = jnp.zeros((2, 16, channels), BF16)

    def fold():
        got_up_w.wait()
        got_up_b.wait()
        fold_w[:, :, up_channels:, :] = jnp.zeros(
            (2, 2, 2 * LANES - up_channels, 4 * channels), BF16
        )
        groups = (((0,), (1, 2)), ((0, 1), (2,)))
        for p in range(2):
            for q in range(2):
                for d in range(2):
                    for g in range(2):
                        parts = [
                            up_w[a, b].astype(F32) for a in groups[p][d] for b in groups[q][g]
                        ]
                        lanes = pl.ds((d * 2 + g) * channels, channels)
                        fold_w[p, q, 0:up_channels, lanes] = sum(parts).astype(BF16)
        offset[...] = up_b[...][None, :]

    core_rows = ((rim, core),)
    rim_rows = ((0, rim), (height - rim, rim))

    def lhs(frame, b, es, blocks):
        first, count = es[0] * channels, len(es) * channels
        parts = [
            taps_1[frame, b + start : b + start + size, :, first : first + count].reshape(
                size * breadth, count
            )
            for start, size in blocks
        ]
        return parts[0] if len(parts) == 1 else jnp.concatenate(parts, axis=0)

    def weight(a, b, es):
        return conv_w[a, b, es[0] : es[-1] + 1].reshape(len(es) * channels, channels)

    def pair(groups, blocks):
        xs, ws = [], []
        for es in groups:
            for b in range(3):
                xs += [lhs(1, b, es, blocks), lhs(2, b, es, blocks)]
                ws += [
                    jnp.concatenate([weight(1, b, es), weight(0, b, es)], axis=1),
                    jnp.concatenate([weight(2, b, es), weight(1, b, es)], axis=1),
                ]
        return dot(jnp.concatenate(xs, axis=1), jnp.concatenate(ws, axis=0))

    def end(source, a, groups, blocks):
        order = [(es, b) for es in groups for b in range(3)]
        return dot(
            jnp.concatenate([lhs(source, b, es, blocks) for es, b in order], axis=1),
            jnp.concatenate([weight(a, b, es) for es, b in order], axis=0),
        )

    ends = ((0, 0), (3, 2))

    def conv_core_middle():
        for copy in got_conv_w[1]:
            copy.wait()
        total[...] = pair([(1,)], core_rows)
        for frame, (source, a) in enumerate(ends):
            lanes = slice(frame * channels, (frame + 1) * channels)
            total[:, lanes] += end(source, a, [(1,)], core_rows)

    def columns_1():
        await_from(state[0], (2, 3))
        place_columns(0)
        for frame in range(4):
            shift(taps_1, frame, 1, height)

    def finish(frame, summed, blocks):
        done = 0
        for start, size in blocks:
            here = pl.ds(start * breadth, size * breadth)
            short = shortcut[frame, start : start + size].reshape(size * breadth, channels)
            part = summed[done : done + size * breadth]
            block_out[frame, here] = (part + short.astype(F32) + conv_b[...][None, :]).astype(BF16)
            done += size * breadth

    def conv_core():
        for e in (0, 2):
            for copy in got_conv_w[e]:
                copy.wait()
        total[...] += pair([(0,), (2,)], core_rows)
        got_shortcut.wait()
        got_conv_b.wait()
        for frame, (source, a) in enumerate(ends):
            lanes = slice(frame * channels, (frame + 1) * channels)
            summed = total[:, lanes] + end(source, a, [(0,), (2,)], core_rows)
            finish(frame, summed, core_rows)

    def rows_1():
        await_from(state[0], (0, 1, 4, 5, 6, 7))
        place_rows(0, taps_1)
        for frame in range(4):
            for at in (0, tall - 1):
                shift(taps_1, frame, at, 1)

    def conv_rim():
        count = 2 * rim * breadth
        total[0:count] = pair([(0, 1, 2)], rim_rows)
        for frame, (source, a) in enumerate(ends):
            lanes = slice(frame * channels, (frame + 1) * channels)
            finish(frame, total[0:count, lanes] + end(source, a, [(0, 1, 2)], rim_rows), rim_rows)

    def time_conv():
        got_cache.wait()
        got_time_w.wait()
        got_time_b.wait()
        past = [cache[frame].reshape(cells, channels) for frame in range(2)]
        stacked = past + [block_out[0], block_out[1]]
        for frame in range(2):
            doubled = dot(
                jnp.concatenate(stacked[frame : frame + 3], axis=1),
                time_w[...].reshape(3 * channels, 2 * channels),
            )
            doubled = doubled + time_b[...][None, :]
            for m in range(2):
                part = doubled[:, m * channels : (m + 1) * channels]
                part = part.reshape(height, breadth, channels)
                taps_2[2 * frame + m, 1 : height + 1, :, middle] = part.astype(BF16)
                hold(2 * frame + m, part)

    def send_2():
        state[1] = send(1, taps_2)

    def up_core():
        for place in (BASE - 1, BASE + breadth):
            for frame in range(4):
                start = (frame * tall + 1) * PITCH + place
                for k in range(chunks):
                    flat[k, pl.ds(start, height, stride=PITCH), :] = jnp.zeros((height, LANES), F32)
        for frame in range(4):
            shift(taps_2, frame, rim, core + 2)
        upsample(taps_2, fold_w, rim, core, fine, 0)

    def receive_2():
        await_from(state[1], range(8))
        flat_fine = fine.reshape(2, 4 * 2 * core * 2 * breadth, LANES)
        for q in range(2):
            values = edge_in[1, q].astype(F32)
            for p in range(2):
                summed = 0.0
                for d in range(2):
                    first = rim + p + d - 1
                    x = jnp.concatenate(
                        [
                            values[frame * height + first : frame * height + first + core]
                            for frame in range(4)
                        ],
                        axis=0,
                    ).astype(BF16)
                    lanes = pl.ds((2 * d + q) * channels, channels)
                    summed = summed + dot_t(x, fold_w[p, q, :, lanes])
                for frame in range(4):
                    start = (frame * 2 * core + p) * 2 * breadth + q * (2 * breadth - 1)
                    spots = pl.ds(start, core, stride=4 * breadth)
                    for k in range(2):
                        flat_fine[k, spots, :] += summed[
                            frame * core : (frame + 1) * core, lanes_of(k)
                        ]
        place_columns(1)
        place_rows(1, taps_2)
        for frame in range(4):
            shift(taps_2, frame, 0, rim + 2)
            shift(taps_2, frame, height - rim, rim + 2)

    def sent():
        for copies in state.values():
            for index, copy in copies.items():
                pl.when(exists[index])(copy.wait_send)

    steps = (
        begin, send_1, outside, fold, conv_core_middle, columns_1, conv_core, rows_1, conv_rim,
        time_conv, send_2, up_core, receive_2, sent,
    )
    for step in steps:
        step()


def upsample(taps, fold_w, first, count, fine, to):
    frames, _, breadth, channels = taps.shape
    channels //= 3
    for p in range(2):
        for q in range(2):
            summed = 0.0
            for d in range(2):
                rows = pl.ds(first + p + d, count)
                x = taps[:, rows, :, q * channels : (q + 2) * channels]
                w = fold_w[p, q, :, 2 * d * channels : 2 * (d + 1) * channels]
                summed = summed + dot_t(x.reshape(frames * count * breadth, 2 * channels), w)
            summed = summed.reshape(frames, count, breadth, 2 * LANES)
            for frame in range(frames):
                for r in range(count):
                    for k in range(2):
                        fine[k, frame, to + 2 * r + p, pl.ds(q, breadth, stride=2), :] = summed[
                            frame, r, :, k * LANES : (k + 1) * LANES
                        ]


def upsample_kernel(dims, taps, fold_w, offset, core_fine, out, fine, fine_out, store_sem):
    height, breadth, channels, up_channels = dims
    rim = height // 6
    core = height - 2 * rim

    def store(index, source, start, to, count):
        for k in range(2):
            lanes = slice(k * LANES, min((k + 1) * LANES, up_channels))
            size = lanes.stop - lanes.start
            values = source[k, :, pl.ds(start, count), :, 0:size]
            values = values + offset[:, lanes].reshape(1, 1, 1, size)
            fine_out[:, pl.ds(to, count), :, lanes] = values.astype(BF16)
        here = pl.ds(to, count)
        copy = pltpu.make_async_copy(fine_out.at[:, here], out.at[:, here], store_sem.at[index])
        copy.start()
        return copy

    stores = [store(0, core_fine, 0, 2 * rim, 2 * core)]
    for index, first in ((1, 0), (2, height - rim)):
        to = 2 * rim * (index - 1)
        upsample(taps, fold_w, first, rim, fine, to)
        stores.append(store(index, fine, to, 2 * first, 2 * rim))
    for copy in stores:
        copy.wait()


def solution(mesh):
    rows, cols = mesh.shape["row"], mesh.shape["col"]

    def on_device(*args):
        _, height, breadth, channels = args[0].shape
        up_channels = args[9].shape[-1]
        tall, chunks = height + 2, channels // LANES
        rim = height // 6
        core = height - 2 * rim
        args = args[:9] + (jnp.swapaxes(args[9], 2, 3), args[10])
        args = [pltpu.with_memory_space_constraint(x, pltpu.HBM) for x in args]
        vmem = pltpu.VMEM
        dma = pltpu.SemaphoreType.DMA
        field = (rows, cols, height, breadth, channels, up_channels)
        taps_shape = (4, tall, breadth, 3 * channels)
        passed = (
            vmem(taps_shape, BF16),
            vmem((2, 2, 2 * LANES, 4 * channels), BF16),
            vmem((1, up_channels), F32),
            vmem((2, 4, 2 * core, 2 * breadth, LANES), F32),
        )
        whole = pl.BlockSpec(memory_space=pltpu.VMEM)
        passed_on = pl.pallas_call(
            lambda *refs: field_kernel(field, *refs),
            out_shape=passed,
            in_specs=[pl.BlockSpec(memory_space=pltpu.HBM)] * len(args),
            out_specs=(whole,) * len(passed),
            scratch_shapes=[
                vmem(taps_shape, BF16),
                vmem((chunks, 4 * tall, PITCH, LANES), F32),
                vmem((2, height, breadth, channels), BF16),
                vmem((2, height, breadth, channels), BF16),
                vmem((2, height, breadth, channels), BF16),
                vmem((3, 3, 3, channels, channels), BF16),
                vmem((3, channels, 2 * channels), BF16),
                vmem((3, 3, up_channels, channels), BF16),
                vmem((channels,), F32),
                vmem((channels,), F32),
                vmem((2 * channels,), F32),
                vmem((up_channels,), F32),
                vmem((core * breadth, 2 * channels), F32),
                vmem((2, height * breadth, channels), BF16),
                vmem((chunks, 2, 4 * height, LANES), F32),
                vmem((2, 2, 4 * height, channels), BF16),
                vmem((2, 2, 4 * height, channels), BF16),
                vmem((4, 16, LANES), F32),
                vmem((2, 4, 16, channels), BF16),
                vmem((2, 4, 16, channels), BF16),
                dma((10,)),
                dma((3, 3)),
                dma((2, 8)),
                dma((2, 8)),
            ],
            compiler_params=pltpu.CompilerParams(
                collective_id=0, has_side_effects=True, vmem_limit_bytes=40 * 2**20
            ),
        )(*args)
        passed_on = [pltpu.with_memory_space_constraint(x, pltpu.VMEM) for x in passed_on]
        fine = (4, 2 * height, 2 * breadth)
        return pl.pallas_call(
            lambda *refs: upsample_kernel((height, breadth, channels, up_channels), *refs),
            out_shape=jax.ShapeDtypeStruct(fine + (up_channels,), BF16),
            in_specs=[whole] * len(passed),
            out_specs=pl.BlockSpec(memory_space=pl.ANY),
            scratch_shapes=[
                vmem((2, 4, 4 * rim, 2 * breadth, LANES), F32),
                vmem(fine + (up_channels,), BF16),
                dma((3,)),
            ],
            compiler_params=pltpu.CompilerParams(vmem_limit_bytes=32 * 2**20),
        )(*passed_on)

    placed = (P(None, "row", "col", None),) * 4 + (P(),) * 7
    return jax.shard_map(
        on_device,
        mesh=mesh,
        in_specs=placed,
        out_specs=P(None, "row", "col", None),
        check_vma=False,
    )
```

time: 41.3 us -> 30.8 us (0.75)
  the two profiles are of different devices: /device:TPU:1 before, /device:TPU:132 now
where the time goes in v2:
time: 30.8 us
  Pallas kernels  30.6 us (99%)
    pallas_call x1, Pallas kernels, on_device(): pl.pallas_call(lambda *refs: field_kernel(field, *refs), out_shape=passed...  27.3 us
    pallas_call x1, Pallas kernels, on_device(): pl.pallas_call(lambda *refs: upsample_kernel((height, breadth, channels,...  3.33 us

profile of v2, /device:TPU:132, one launch (start us, length us, event | category | flops | bytes accessed | tf_op | source)
XLA Modules:
  0.0 30.8 jit_solution(14375497641377644370)
XLA Ops:
  0.0 27.3 %shard_map.109 = (bf16[4,26,16,1152]{3,2,1,0:T(8,128)(2,1)S(1)}, bf16[2,2,256,1536]{3,2,1,0:T(8,128)(2,1)S(1)}, f32[1,192]{1,0:T(1,128)S(1)}, f32[2,4,32,32,128]{4,3,2,1,0:T(8,128)S(1)}) custom-call(bf16[2,24,16,384]{3,2,1,0:T(8,128)(2,1)} %refs_0_.1, bf16[2,24,16,384]{3,2,1,0:T(8,128)(2,1)} %refs_1_.1, bf16[2,24,16,384]{3,2,1,0:T(8,128)(2,1)} %refs_2_.1, ...), custom_call_target="tpu_custom_call" | custom-call | tf_op jit(solution)/shard_map/pallas_call | solution.py:497
  27.3 3.3 %shard_map.110 = bf16[4,48,32,192]{3,2,1,0:T(8,128)(2,1)} custom-call(bf16[4,26,16,1152]{3,2,1,0:T(8,128)(2,1)S(1)} %get-tuple-element.9.refs_0_, bf16[2,2,256,1536]{3,2,1,0:T(8,128)(2,1)S(1)} %get-tuple-element.10.refs_1_, f32[1,192]{1,0:T(1,128)S(1)} %get-tuple-element.11.refs_2_, f32[2,4,32,32,128]{4,3,2,1,0:T(8,128)S(1)} %get-tuple-element.12.refs_3_), custom_call_target="tpu_custom_call" | custom-call | tf_op jit(solution)/shard_map/pallas_call | solution.py:534

commit v3 on v2

--- a/solution.py
+++ b/solution.py
@@ -50,10 +50,15 @@
     time_b,
     up_b,
     total,
+    past,
     block_out,
     edge_f32,
     edge_out,
     edge_in,
+    core_out,
+    core_in,
+    rim_out,
+    rim_in,
     corner_f32,
     corner_out,
     corner_in,
@@ -86,13 +91,14 @@
             for a in range(3)
         ]
         if e == 1:
+            got_cache = load(time_cache, cache, load_sem.at[6])
+            got_time_w = load(time_weight, time_w, load_sem.at[7])
+            got_time_b = load(time_bias, time_b, load_sem.at[8])
+        if e == 0:
             got_up_w = load(upsample_weight, up_w, load_sem.at[3])
             got_up_b = load(upsample_bias, up_b, load_sem.at[9])
     got_shortcut = load(block_input, shortcut, load_sem.at[4])
     got_conv_b = load(conv_bias, conv_b, load_sem.at[5])
-    got_cache = load(time_cache, cache, load_sem.at[6])
-    got_time_w = load(time_weight, time_w, load_sem.at[7])
-    got_time_b = load(time_bias, time_b, load_sem.at[8])
 
     steps_to = ((-1, 0), (1, 0), (0, -1), (0, 1), (-1, -1), (-1, 1), (1, -1), (1, 1))
     opposite = (1, 0, 3, 2, 7, 6, 5, 4)
@@ -118,7 +124,6 @@
 
     chunks = channels // LANES
     flat = wide.reshape(chunks, 4 * tall * PITCH, LANES)
-    edges = edge_f32.reshape(chunks, 2 * 4 * height, LANES)
 
     def lanes_of(k):
         return slice(k * LANES, (k + 1) * LANES)
@@ -128,54 +133,62 @@
         for k in range(chunks):
             wide[k, here, BASE : BASE + breadth, :] = values[:, :, lanes_of(k)]
 
-    def send(turn, taps):
+    def pick_edges(blocks, target):
+        count = sum(size for _, size in blocks)
         for side, place in ((0, BASE), (1, BASE + breadth - 1)):
-            for frame in range(4):
-                start = (frame * tall + 1) * PITCH + place
-                for k in range(chunks):
-                    edge_f32[k, side, frame * height : (frame + 1) * height, :] = flat[
-                        k, pl.ds(start, height, stride=PITCH), :
-                    ]
             for k in range(chunks):
-                edge_out[turn, side, :, lanes_of(k)] = edge_f32[k, side].astype(BF16)
+                for frame in range(4):
+                    to = frame * count
+                    for first, size in blocks:
+                        start = (frame * tall + 1 + first) * PITCH + place
+                        edge_f32[k, side, to : to + size, :] = flat[
+                            k, pl.ds(start, size, stride=PITCH), :
+                        ]
+                        to += size
+                target[side, :, lanes_of(k)] = edge_f32[k, side, 0 : 4 * count].astype(BF16)
+
+    def pick_corners(target):
         for k in range(chunks):
             for corner in range(4):
-                start = (corner % 2) * 4 * height + (corner // 2) * (height - 1)
-                corner_f32[corner, 0:4, :] = edges[k, pl.ds(start, 4, stride=height), :]
-            corner_out[turn, :, :, lanes_of(k)] = corner_f32[...].astype(BF16)
+                place = BASE + (breadth - 1) * (corner % 2)
+                for frame in range(4):
+                    start = (frame * tall + 1 + (height - 1) * (corner // 2)) * PITCH + place
+                    corner_f32[corner, frame : frame + 1, :] = flat[k, start : start + 1, :]
+            target[:, :, lanes_of(k)] = corner_f32[...].astype(BF16)
+
+    def send(turn, index, source, target, sem):
         if not linked:
-            return {}
-        if turn == 0:
-            around = 1 + one(has[-1, 0]) + one(has[1, 0])
-            across = 1 + one(has[0, -1]) + one(has[0, 1])
-            pl.semaphore_wait(barrier, around * across - 1)
-        pairs = [
-            (taps.at[:, 1, :, middle], taps.at[:, tall - 1, :, middle]),
-            (taps.at[:, height, :, middle], taps.at[:, 0, :, middle]),
-            (edge_out.at[turn, 0], edge_in.at[turn, 1]),
-            (edge_out.at[turn, 1], edge_in.at[turn, 0]),
-            (corner_out.at[turn, 0], corner_in.at[turn, 3]),
-            (corner_out.at[turn, 1], corner_in.at[turn, 2]),
-            (corner_out.at[turn, 2], corner_in.at[turn, 1]),
-            (corner_out.at[turn, 3], corner_in.at[turn, 0]),
-        ]
-        copies = {}
-        for index in (2, 3, 0, 1, 4, 5, 6, 7):
-            down, along = steps_to[index]
-            copies[index] = pltpu.make_async_remote_copy(
-                src_ref=pairs[index][0],
-                dst_ref=pairs[index][1],
-                send_sem=send_sem.at[turn, index],
-                recv_sem=recv_sem.at[turn, index],
-                device_id=(row + down, col + along),
-                device_id_type=MESH,
-            )
-            pl.when(exists[index])(copies[index].start)
-        return copies
-
-    def await_from(copies, indices):
-        for index in indices if linked else ():
-            pl.when(exists[opposite[index]])(copies[index].wait_recv)
+            return
+        down, along = steps_to[index]
+        copy = pltpu.make_async_remote_copy(
+            src_ref=source,
+            dst_ref=target,
+            send_sem=send_sem.at[turn, sem],
+            recv_sem=recv_sem.at[turn, sem],
+            device_id=(row + down, col + along),
+            device_id_type=MESH,
+        )
+        pl.when(exists[index])(copy.start)
+        sent_copies.append((index, copy))
+        state[turn, sem] = (index, copy)
+
+    def send_edges(turn, source, target, sem):
+        send(turn, 2, source.at[0], target.at[1], sem)
+        send(turn, 3, source.at[1], target.at[0], sem + 1)
+
+    def send_rows(turn, taps):
+        send(turn, 0, taps.at[:, 1, :, middle], taps.at[:, tall - 1, :, middle], 0)
+        send(turn, 1, taps.at[:, height, :, middle], taps.at[:, 0, :, middle], 1)
+
+    def send_corners(turn):
+        for corner in range(4):
+            source, target = corner_out.at[turn, corner], corner_in.at[turn, 3 - corner]
+            send(turn, 4 + corner, source, target, 4 + corner)
+
+    def await_from(turn, sems):
+        for sem in sems if linked else ():
+            index, copy = state[turn, sem]
+            pl.when(exists[opposite[index]])(copy.wait_recv)
 
     def shift(taps, frame, first, count):
         here = pl.ds(frame * tall + first, count)
@@ -185,15 +198,19 @@
                 shifted = wide[k, here, start : start + breadth, :].astype(BF16)
                 taps[frame, first : first + count, :, lanes_of(e * chunks + k)] = shifted
 
-    def place_columns(turn):
+    def place_columns(source, blocks):
+        count = sum(size for _, size in blocks)
         for side, place in ((0, BASE - 1), (1, BASE + breadth)):
-            values = edge_in[turn, side].astype(F32)
+            values = source[side].astype(F32)
             for frame in range(4):
-                start = (frame * tall + 1) * PITCH + place
-                for k in range(chunks):
-                    flat[k, pl.ds(start, height, stride=PITCH), :] = values[
-                        frame * height : (frame + 1) * height, lanes_of(k)
-                    ]
+                done = frame * count
+                for first, size in blocks:
+                    start = (frame * tall + 1 + first) * PITCH + place
+                    for k in range(chunks):
+                        flat[k, pl.ds(start, size, stride=PITCH), :] = values[
+                            done : done + size, lanes_of(k)
+                        ]
+                    done += size
 
     def place_rows(turn, taps):
         for end, at in ((0, 0), (1, tall - 1)):
@@ -208,7 +225,10 @@
                     for k in range(chunks):
                         flat[k, spot : spot + 1, :] = values[frame : frame + 1, lanes_of(k)]
 
-    state = {}
+    state, sent_copies = {}, []
+    all_rows = ((0, height),)
+    core_rows = ((rim, core),)
+    rim_rows = ((0, rim), (height - rim, rim))
 
     def begin():
         got_inner.wait()
@@ -225,8 +245,18 @@
             hold(frame, taps_1[frame, 1 : height + 1, :, middle].astype(F32))
         corner_f32[...] = jnp.zeros_like(corner_f32)
 
-    def send_1():
-        state[0] = send(0, taps_1)
+    def send_columns_1():
+        pick_edges(all_rows, edge_out)
+        if linked:
+            around = 1 + one(has[-1, 0]) + one(has[1, 0])
+            across = 1 + one(has[0, -1]) + one(has[0, 1])
+            pl.semaphore_wait(barrier, around * across - 1)
+        send_edges(0, edge_out, edge_in, 2)
+
+    def send_rows_1():
+        pick_corners(corner_out.at[0])
+        send_rows(0, taps_1)
+        send_corners(0)
 
     def outside():
         for end, at in ((-1, 0), (1, tall - 1)):
@@ -240,7 +270,8 @@
 
             @pl.when(jnp.logical_not(has[0, along]))
             def _():
-                edge_in[:, side] = jnp.zeros((2, 4 * height, channels), BF16)
+                for target in (edge_in, core_in, rim_in):
+                    target[side] = jnp.zeros(target.shape[1:], BF16)
 
         for corner in range(4):
 
@@ -266,9 +297,6 @@
                         fold_w[p, q, 0:up_channels, lanes] = sum(parts).astype(BF16)
         offset[...] = up_b[...][None, :]
 
-    core_rows = ((rim, core),)
-    rim_rows = ((0, rim), (height - rim, rim))
-
     def lhs(frame, b, es, blocks):
         first, count = es[0] * channels, len(es) * channels
         parts = [
@@ -311,8 +339,8 @@
             total[:, lanes] += end(source, a, [(1,)], core_rows)
 
     def columns_1():
-        await_from(state[0], (2, 3))
-        place_columns(0)
+        await_from(0, (2, 3))
+        place_columns(edge_in, all_rows)
         for frame in range(4):
             shift(taps_1, frame, 1, height)
 
@@ -338,7 +366,7 @@
             finish(frame, summed, core_rows)
 
     def rows_1():
-        await_from(state[0], (0, 1, 4, 5, 6, 7))
+        await_from(0, (0, 1, 4, 5, 6, 7))
         place_rows(0, taps_1)
         for frame in range(4):
             for at in (0, tall - 1):
@@ -351,26 +379,50 @@
             lanes = slice(frame * channels, (frame + 1) * channels)
             finish(frame, total[0:count, lanes] + end(source, a, [(0, 1, 2)], rim_rows), rim_rows)
 
-    def time_conv():
+    def time_weights(first):
+        return time_w[first:].reshape((3 - first) * channels, 2 * channels)
+
+    def time_past():
         got_cache.wait()
         got_time_w.wait()
         got_time_b.wait()
-        past = [cache[frame].reshape(cells, channels) for frame in range(2)]
-        stacked = past + [block_out[0], block_out[1]]
-        for frame in range(2):
-            doubled = dot(
-                jnp.concatenate(stacked[frame : frame + 3], axis=1),
-                time_w[...].reshape(3 * channels, 2 * channels),
-            )
-            doubled = doubled + time_b[...][None, :]
-            for m in range(2):
-                part = doubled[:, m * channels : (m + 1) * channels]
-                part = part.reshape(height, breadth, channels)
-                taps_2[2 * frame + m, 1 : height + 1, :, middle] = part.astype(BF16)
-                hold(2 * frame + m, part)
-
-    def send_2():
-        state[1] = send(1, taps_2)
+        old = [cache[frame].reshape(cells, channels) for frame in range(2)]
+        kernel_0 = time_w[0:2].reshape(2 * channels, 2 * channels)
+        past[0] = dot(jnp.concatenate(old, axis=1), kernel_0) + time_b[...][None, :]
+        past[1] = dot(old[1], time_w[0]) + time_b[...][None, :]
+
+    def time_conv(blocks):
+        for first, size in blocks:
+            here = pl.ds(first * breadth, size * breadth)
+            new = [block_out[frame, here] for frame in range(2)]
+            for frame in range(2):
+                x = jnp.concatenate(new[: frame + 1], axis=1)
+                doubled = past[frame, here] + dot(x, time_weights(2 - frame))
+                for m in range(2):
+                    part = doubled[:, m * channels : (m + 1) * channels]
+                    part = part.reshape(size, breadth, channels)
+                    at = 2 * frame + m
+                    taps_2[at, 1 + first : 1 + first + size, :, middle] = part.astype(BF16)
+                    rows_of = pl.ds(at * tall + 1 + first, size)
+                    for k in range(chunks):
+                        wide[k, rows_of, BASE : BASE + breadth, :] = part[:, :, lanes_of(k)]
+
+    def time_core():
+        time_conv(core_rows)
+
+    def send_core_2():
+        pick_edges(core_rows, core_out)
+        send_edges(1, core_out, core_in, 2)
+
+    def time_rim():
+        time_conv(rim_rows)
+
+    def send_rim_2():
+        send_rows(1, taps_2)
+        pick_edges(rim_rows, rim_out)
+        send_edges(1, rim_out, rim_in, 8)
+        pick_corners(corner_out.at[1])
+        send_corners(1)
 
     def up_core():
         for place in (BASE - 1, BASE + breadth):
@@ -383,18 +435,28 @@
         upsample(taps_2, fold_w, rim, core, fine, 0)
 
     def receive_2():
-        await_from(state[1], range(8))
+        await_from(1, range(10))
+        place_columns(core_in, core_rows)
+        place_columns(rim_in, rim_rows)
         flat_fine = fine.reshape(2, 4 * 2 * core * 2 * breadth, LANES)
         for q in range(2):
-            values = edge_in[1, q].astype(F32)
+            place = BASE - 1 + q * (breadth + 1)
             for p in range(2):
                 summed = 0.0
                 for d in range(2):
                     first = rim + p + d - 1
                     x = jnp.concatenate(
                         [
-                            values[frame * height + first : frame * height + first + core]
-                            for frame in range(4)
+                            jnp.concatenate(
+                                [
+                                    flat[k, pl.ds(start, core, stride=PITCH), :]
+                                    for k in range(chunks)
+                                ],
+                                axis=1,
+                            )
+                            for start in [
+                                (frame * tall + 1 + first) * PITCH + place for frame in range(4)
+                            ]
                         ],
                         axis=0,
                     ).astype(BF16)
@@ -407,20 +469,19 @@
                         flat_fine[k, spots, :] += summed[
                             frame * core : (frame + 1) * core, lanes_of(k)
                         ]
-        place_columns(1)
         place_rows(1, taps_2)
         for frame in range(4):
             shift(taps_2, frame, 0, rim + 2)
             shift(taps_2, frame, height - rim, rim + 2)
 
     def sent():
-        for copies in state.values():
-            for index, copy in copies.items():
-                pl.when(exists[index])(copy.wait_send)
+        for index, copy in sent_copies:
+            pl.when(exists[index])(copy.wait_send)
 
     steps = (
-        begin, send_1, outside, fold, conv_core_middle, columns_1, conv_core, rows_1, conv_rim,
-        time_conv, send_2, up_core, receive_2, sent,
+        begin, send_columns_1, outside, conv_core_middle, send_rows_1, time_past, fold, columns_1,
+        conv_core, time_core, send_core_2, rows_1, conv_rim, time_rim, send_rim_2, up_core,
+        receive_2, sent,
     )
     for step in steps:
         step()
@@ -513,17 +574,22 @@
                 vmem((2 * channels,), F32),
                 vmem((up_channels,), F32),
                 vmem((core * breadth, 2 * channels), F32),
+                vmem((2, height * breadth, 2 * channels), F32),
                 vmem((2, height * breadth, channels), BF16),
                 vmem((chunks, 2, 4 * height, LANES), F32),
-                vmem((2, 2, 4 * height, channels), BF16),
-                vmem((2, 2, 4 * height, channels), BF16),
+                vmem((2, 4 * height, channels), BF16),
+                vmem((2, 4 * height, channels), BF16),
+                vmem((2, 4 * core, channels), BF16),
+                vmem((2, 4 * core, channels), BF16),
+                vmem((2, 8 * rim, channels), BF16),
+                vmem((2, 8 * rim, channels), BF16),
                 vmem((4, 16, LANES), F32),
                 vmem((2, 4, 16, channels), BF16),
                 vmem((2, 4, 16, channels), BF16),
                 dma((10,)),
                 dma((3, 3)),
-                dma((2, 8)),
-                dma((2, 8)),
+                dma((2, 10)),
+                dma((2, 10)),
             ],
             compiler_params=pltpu.CompilerParams(
                 collective_id=0, has_side_effects=True, vmem_limit_bytes=40 * 2**20

time: 30.8 us -> 29 us (0.942)
  Pallas kernels: 30.6 us -> 28.8 us
    pallas_call x1, Pallas kernels: 27.3 us -> 25.4 us  [on_device(): pl.pallas_call(lambda *refs: field_kernel(field, *refs), out_shape=passed...]
where the time goes in v3:
time: 29 us; the launch traced here: 28.9 us
  Pallas kernels  28.8 us (99%)
    pallas_call x1, Pallas kernels, on_device(): pl.pallas_call(lambda *refs: field_kernel(field, *refs), out_shape=passed...  25.4 us
    pallas_call x1, Pallas kernels, on_device(): pl.pallas_call(lambda *refs: upsample_kernel((height, breadth, channels,...  3.33 us

profile of v3, /device:TPU:132, one launch (start us, length us, event | category | flops | bytes accessed | tf_op | source)
XLA Modules:
  0.0 28.9 jit_solution(14639645983124115792)
XLA Ops:
  0.0 25.4 %shard_map.109 = (bf16[4,26,16,1152]{3,2,1,0:T(8,128)(2,1)S(1)}, bf16[2,2,256,1536]{3,2,1,0:T(8,128)(2,1)S(1)}, f32[1,192]{1,0:T(1,128)S(1)}, f32[2,4,32,32,128]{4,3,2,1,0:T(8,128)S(1)}) custom-call(bf16[2,24,16,384]{3,2,1,0:T(8,128)(2,1)} %refs_0_.1, bf16[2,24,16,384]{3,2,1,0:T(8,128)(2,1)} %refs_1_.1, bf16[2,24,16,384]{3,2,1,0:T(8,128)(2,1)} %refs_2_.1, ...), custom_call_target="tpu_custom_call" | custom-call | tf_op jit(solution)/shard_map/pallas_call | solution.py:558
  25.4 3.3 %shard_map.110 = bf16[4,48,32,192]{3,2,1,0:T(8,128)(2,1)} custom-call(bf16[4,26,16,1152]{3,2,1,0:T(8,128)(2,1)S(1)} %get-tuple-element.9.refs_0_, bf16[2,2,256,1536]{3,2,1,0:T(8,128)(2,1)S(1)} %get-tuple-element.10.refs_1_, f32[1,192]{1,0:T(1,128)S(1)} %get-tuple-element.11.refs_2_, f32[2,4,32,32,128]{4,3,2,1,0:T(8,128)S(1)} %get-tuple-element.12.refs_3_), custom_call_target="tpu_custom_call" | custom-call | tf_op jit(solution)/shard_map/pallas_call | solution.py:600

commit v4 on v3

--- a/solution.py
+++ b/solution.py
@@ -49,6 +49,9 @@
     conv_b,
     time_b,
     up_b,
+    gain_row,
+    conv_b_row,
+    time_b_row,
     total,
     past,
     block_out,
@@ -83,6 +86,9 @@
 
     got_inner = load(block_inner, inner, load_sem.at[0])
     got_gain = load(norm_gain, gain, load_sem.at[2])
+    got_conv_b = load(conv_bias, conv_b, load_sem.at[5])
+    got_time_b = load(time_bias, time_b, load_sem.at[8])
+    got_up_b = load(upsample_bias, up_b, load_sem.at[9])
     got_conv_cache = load(conv_cache, taps_1.at[0:2, 1 : height + 1, :, middle], load_sem.at[1])
     got_conv_w = [None] * 3
     for e in (1, 0, 2):
@@ -93,12 +99,9 @@
         if e == 1:
             got_cache = load(time_cache, cache, load_sem.at[6])
             got_time_w = load(time_weight, time_w, load_sem.at[7])
-            got_time_b = load(time_bias, time_b, load_sem.at[8])
         if e == 0:
             got_up_w = load(upsample_weight, up_w, load_sem.at[3])
-            got_up_b = load(upsample_bias, up_b, load_sem.at[9])
     got_shortcut = load(block_input, shortcut, load_sem.at[4])
-    got_conv_b = load(conv_bias, conv_b, load_sem.at[5])
 
     steps_to = ((-1, 0), (1, 0), (0, -1), (0, 1), (-1, -1), (-1, 1), (1, -1), (1, 1))
     opposite = (1, 0, 3, 2, 7, 6, 5, 4)
@@ -233,10 +236,11 @@
     def begin():
         got_inner.wait()
         got_gain.wait()
+        gain_row[...] = gain[...][None, :]
         for frame in range(2):
             values = inner[frame].reshape(cells, channels).astype(F32)
             mean = jnp.sum(values * values, axis=-1, keepdims=True) * (1.0 / channels)
-            normed = values * lax.rsqrt(mean + EPSILON) * gain[...][None, :]
+            normed = values * lax.rsqrt(mean + EPSILON) * gain_row[...]
             active = (normed * jax.nn.sigmoid(normed)).reshape(height, breadth, channels)
             taps_1[2 + frame, 1 : height + 1, :, middle] = active.astype(BF16)
             hold(2 + frame, active)
@@ -259,6 +263,12 @@
         send_corners(0)
 
     def outside():
+        got_conv_b.wait()
+        conv_b_row[...] = conv_b[...][None, :]
+        got_time_b.wait()
+        time_b_row[...] = time_b[...][None, :]
+        got_up_b.wait()
+        offset[...] = up_b[...][None, :]
         for end, at in ((-1, 0), (1, tall - 1)):
 
             @pl.when(jnp.logical_not(has[end, 0]))
@@ -280,22 +290,22 @@
                 corner_in[:, corner] = jnp.zeros((2, 16, channels), BF16)
 
     def fold():
-        got_up_w.wait()
-        got_up_b.wait()
         fold_w[:, :, up_channels:, :] = jnp.zeros(
             (2, 2, 2 * LANES - up_channels, 4 * channels), BF16
         )
-        groups = (((0,), (1, 2)), ((0, 1), (2,)))
+        parts = [[up_w[a, b].astype(F32) for b in range(3)] for a in range(3)]
+
+        def folded(x):
+            return ((x[0], x[1] + x[2]), (x[0] + x[1], x[2]))
+
+        by_row = [folded([parts[a][b] for a in range(3)]) for b in range(3)]
         for p in range(2):
-            for q in range(2):
-                for d in range(2):
+            for d in range(2):
+                by_both = folded([by_row[b][p][d] for b in range(3)])
+                for q in range(2):
                     for g in range(2):
-                        parts = [
-                            up_w[a, b].astype(F32) for a in groups[p][d] for b in groups[q][g]
-                        ]
                         lanes = pl.ds((d * 2 + g) * channels, channels)
-                        fold_w[p, q, 0:up_channels, lanes] = sum(parts).astype(BF16)
-        offset[...] = up_b[...][None, :]
+                        fold_w[p, q, 0:up_channels, lanes] = by_both[q][g].astype(BF16)
 
     def lhs(frame, b, es, blocks):
         first, count = es[0] * channels, len(es) * channels
@@ -341,7 +351,7 @@
     def columns_1():
         await_from(0, (2, 3))
         place_columns(edge_in, all_rows)
-        for frame in range(4):
+        for frame in (1, 2):
             shift(taps_1, frame, 1, height)
 
     def finish(frame, summed, blocks):
@@ -350,16 +360,19 @@
             here = pl.ds(start * breadth, size * breadth)
             short = shortcut[frame, start : start + size].reshape(size * breadth, channels)
             part = summed[done : done + size * breadth]
-            block_out[frame, here] = (part + short.astype(F32) + conv_b[...][None, :]).astype(BF16)
+            block_out[frame, here] = (part + short.astype(F32) + conv_b_row[...]).astype(BF16)
             done += size * breadth
 
     def conv_core():
         for e in (0, 2):
             for copy in got_conv_w[e]:
                 copy.wait()
+        got_shortcut.wait()
+        got_up_w.wait()
+        for frame in (0, 3):
+            shift(taps_1, frame, 1, height)
+        fold()
         total[...] += pair([(0,), (2,)], core_rows)
-        got_shortcut.wait()
-        got_conv_b.wait()
         for frame, (source, a) in enumerate(ends):
             lanes = slice(frame * channels, (frame + 1) * channels)
             summed = total[:, lanes] + end(source, a, [(0,), (2,)], core_rows)
@@ -385,11 +398,10 @@
     def time_past():
         got_cache.wait()
         got_time_w.wait()
-        got_time_b.wait()
         old = [cache[frame].reshape(cells, channels) for frame in range(2)]
         kernel_0 = time_w[0:2].reshape(2 * channels, 2 * channels)
-        past[0] = dot(jnp.concatenate(old, axis=1), kernel_0) + time_b[...][None, :]
-        past[1] = dot(old[1], time_w[0]) + time_b[...][None, :]
+        past[0] = dot(jnp.concatenate(old, axis=1), kernel_0) + time_b_row[...]
+        past[1] = dot(old[1], time_w[0]) + time_b_row[...]
 
     def time_conv(blocks):
         for first, size in blocks:
@@ -479,7 +491,7 @@
             pl.when(exists[index])(copy.wait_send)
 
     steps = (
-        begin, send_columns_1, outside, conv_core_middle, send_rows_1, time_past, fold, columns_1,
+        begin, send_columns_1, outside, conv_core_middle, send_rows_1, time_past, columns_1,
         conv_core, time_core, send_core_2, rows_1, conv_rim, time_rim, send_rim_2, up_core,
         receive_2, sent,
     )
@@ -573,6 +585,9 @@
                 vmem((channels,), F32),
                 vmem((2 * channels,), F32),
                 vmem((up_channels,), F32),
+                vmem((1, channels), F32),
+                vmem((1, channels), F32),
+                vmem((1, 2 * channels), F32),
                 vmem((core * breadth, 2 * channels), F32),
                 vmem((2, height * breadth, 2 * channels), F32),
                 vmem((2, height * breadth, channels), BF16),

time: 29 us -> 28.6 us (0.986)
  Pallas kernels: 28.8 us -> 28.4 us
    pallas_call x1, Pallas kernels: 25.4 us -> 25 us  [on_device(): pl.pallas_call(lambda *refs: field_kernel(field, *refs), out_shape=passed...]
where the time goes in v4:
time: 28.6 us; the launch traced here: 28.5 us
  Pallas kernels  28.4 us (99%)
    pallas_call x1, Pallas kernels, on_device(): pl.pallas_call(lambda *refs: field_kernel(field, *refs), out_shape=passed...  25 us
    pallas_call x1, Pallas kernels, on_device(): pl.pallas_call(lambda *refs: upsample_kernel((height, breadth, channels,...  3.33 us

profile of v4, /device:TPU:132, one launch (start us, length us, event | category | flops | bytes accessed | tf_op | source)
XLA Modules:
  0.0 28.5 jit_solution(15140182604883762876)
XLA Ops:
  0.0 25.0 %shard_map.109 = (bf16[4,26,16,1152]{3,2,1,0:T(8,128)(2,1)S(1)}, bf16[2,2,256,1536]{3,2,1,0:T(8,128)(2,1)S(1)}, f32[1,192]{1,0:T(1,128)S(1)}, f32[2,4,32,32,128]{4,3,2,1,0:T(8,128)S(1)}) custom-call(bf16[2,24,16,384]{3,2,1,0:T(8,128)(2,1)} %refs_0_.1, bf16[2,24,16,384]{3,2,1,0:T(8,128)(2,1)} %refs_1_.1, bf16[2,24,16,384]{3,2,1,0:T(8,128)(2,1)} %refs_2_.1, ...), custom_call_target="tpu_custom_call" | custom-call | tf_op jit(solution)/shard_map/pallas_call | solution.py:570
  25.0 3.3 %shard_map.110 = bf16[4,48,32,192]{3,2,1,0:T(8,128)(2,1)} custom-call(bf16[4,26,16,1152]{3,2,1,0:T(8,128)(2,1)S(1)} %get-tuple-element.9.refs_0_, bf16[2,2,256,1536]{3,2,1,0:T(8,128)(2,1)S(1)} %get-tuple-element.10.refs_1_, f32[1,192]{1,0:T(1,128)S(1)} %get-tuple-element.11.refs_2_, f32[2,4,32,32,128]{4,3,2,1,0:T(8,128)S(1)} %get-tuple-element.12.refs_3_), custom_call_target="tpu_custom_call" | custom-call | tf_op jit(solution)/shard_map/pallas_call | solution.py:615

commit v5 on v4

--- a/solution.py
+++ b/solution.py
@@ -53,6 +53,7 @@
     conv_b_row,
     time_b_row,
     total,
+    total_rim,
     past,
     block_out,
     edge_f32,
@@ -151,13 +152,14 @@
                 target[side, :, lanes_of(k)] = edge_f32[k, side, 0 : 4 * count].astype(BF16)
 
     def pick_corners(target):
-        for k in range(chunks):
-            for corner in range(4):
-                place = BASE + (breadth - 1) * (corner % 2)
-                for frame in range(4):
-                    start = (frame * tall + 1 + (height - 1) * (corner // 2)) * PITCH + place
-                    corner_f32[corner, frame : frame + 1, :] = flat[k, start : start + 1, :]
-            target[:, :, lanes_of(k)] = corner_f32[...].astype(BF16)
+        for corner in range(4):
+            place = BASE + (breadth - 1) * (corner % 2)
+            for frame in range(4):
+                start = (frame * tall + 1 + (height - 1) * (corner // 2)) * PITCH + place
+                for k in range(chunks):
+                    to = k * 4 + frame
+                    corner_f32[corner, to : to + 1, :] = flat[k, start : start + 1, :]
+        target[...] = corner_f32[...].astype(BF16)
 
     def send(turn, index, source, target, sem):
         if not linked:
@@ -226,7 +228,7 @@
                 for frame in range(4):
                     spot = (frame * tall + at) * PITCH + place
                     for k in range(chunks):
-                        flat[k, spot : spot + 1, :] = values[frame : frame + 1, lanes_of(k)]
+                        flat[k, spot : spot + 1, :] = values[k * 4 + frame : k * 4 + frame + 1]
 
     state, sent_copies = {}, []
     all_rows = ((0, height),)
@@ -287,7 +289,7 @@
 
             @pl.when(jnp.logical_not(exists[4 + corner]))
             def _():
-                corner_in[:, corner] = jnp.zeros((2, 16, channels), BF16)
+                corner_in[:, corner] = jnp.zeros((2, 16, LANES), BF16)
 
     def fold():
         fold_w[:, :, up_channels:, :] = jnp.zeros(
@@ -340,10 +342,12 @@
 
     ends = ((0, 0), (3, 2))
 
-    def conv_core_middle():
+    def core_middle_pair():
         for copy in got_conv_w[1]:
             copy.wait()
         total[...] = pair([(1,)], core_rows)
+
+    def core_middle_ends():
         for frame, (source, a) in enumerate(ends):
             lanes = slice(frame * channels, (frame + 1) * channels)
             total[:, lanes] += end(source, a, [(1,)], core_rows)
@@ -363,7 +367,7 @@
             block_out[frame, here] = (part + short.astype(F32) + conv_b_row[...]).astype(BF16)
             done += size * breadth
 
-    def conv_core():
+    def core_pair():
         for e in (0, 2):
             for copy in got_conv_w[e]:
                 copy.wait()
@@ -373,6 +377,8 @@
             shift(taps_1, frame, 1, height)
         fold()
         total[...] += pair([(0,), (2,)], core_rows)
+
+    def core_ends():
         for frame, (source, a) in enumerate(ends):
             lanes = slice(frame * channels, (frame + 1) * channels)
             summed = total[:, lanes] + end(source, a, [(0,), (2,)], core_rows)
@@ -386,11 +392,11 @@
                 shift(taps_1, frame, at, 1)
 
     def conv_rim():
-        count = 2 * rim * breadth
-        total[0:count] = pair([(0, 1, 2)], rim_rows)
+        total_rim[...] = pair([(0, 1, 2)], rim_rows)
         for frame, (source, a) in enumerate(ends):
             lanes = slice(frame * channels, (frame + 1) * channels)
-            finish(frame, total[0:count, lanes] + end(source, a, [(0, 1, 2)], rim_rows), rim_rows)
+            summed = total_rim[:, lanes] + end(source, a, [(0, 1, 2)], rim_rows)
+            finish(frame, summed, rim_rows)
 
     def time_weights(first):
         return time_w[first:].reshape((3 - first) * channels, 2 * channels)
@@ -491,9 +497,9 @@
             pl.when(exists[index])(copy.wait_send)
 
     steps = (
-        begin, send_columns_1, outside, conv_core_middle, send_rows_1, time_past, columns_1,
-        conv_core, time_core, send_core_2, rows_1, conv_rim, time_rim, send_rim_2, up_core,
-        receive_2, sent,
+        begin, send_columns_1, outside, core_middle_pair, send_rows_1, core_middle_ends, time_past,
+        columns_1, core_pair, rows_1, conv_rim, time_rim, send_rim_2, core_ends, time_core,
+        send_core_2, up_core, receive_2, sent,
     )
     for step in steps:
         step()
@@ -589,6 +595,7 @@
                 vmem((1, channels), F32),
                 vmem((1, 2 * channels), F32),
                 vmem((core * breadth, 2 * channels), F32),
+                vmem((2 * rim * breadth, 2 * channels), F32),
                 vmem((2, height * breadth, 2 * channels), F32),
                 vmem((2, height * breadth, channels), BF16),
                 vmem((chunks, 2, 4 * height, LANES), F32),
@@ -599,8 +606,8 @@
                 vmem((2, 8 * rim, channels), BF16),
                 vmem((2, 8 * rim, channels), BF16),
                 vmem((4, 16, LANES), F32),
-                vmem((2, 4, 16, channels), BF16),
-                vmem((2, 4, 16, channels), BF16),
+                vmem((2, 4, 16, LANES), BF16),
+                vmem((2, 4, 16, LANES), BF16),
                 dma((10,)),
                 dma((3, 3)),
                 dma((2, 10)),

time: 28.6 us -> 28.5 us (level)
  the two profiles are of different devices: /device:TPU:132 before, /device:TPU:107 now
where the time goes in v5:
time: 28.5 us
  Pallas kernels  28.3 us (99%)
    pallas_call x1, Pallas kernels, on_device(): pl.pallas_call(lambda *refs: field_kernel(field, *refs), out_shape=passed...  24.9 us
    pallas_call x1, Pallas kernels, on_device(): pl.pallas_call(lambda *refs: upsample_kernel((height, breadth, channels,...  3.34 us

profile of v5, /device:TPU:107, one launch (start us, length us, event | category | flops | bytes accessed | tf_op | source)
XLA Modules:
  0.0 28.5 jit_solution(2553753960648498399)
XLA Ops:
  0.0 24.9 %shard_map.109 = (bf16[4,26,16,1152]{3,2,1,0:T(8,128)(2,1)S(1)}, bf16[2,2,256,1536]{3,2,1,0:T(8,128)(2,1)S(1)}, f32[1,192]{1,0:T(1,128)S(1)}, f32[2,4,32,32,128]{4,3,2,1,0:T(8,128)S(1)}) custom-call(bf16[2,24,16,384]{3,2,1,0:T(8,128)(2,1)} %refs_0_.1, bf16[2,24,16,384]{3,2,1,0:T(8,128)(2,1)} %refs_1_.1, bf16[2,24,16,384]{3,2,1,0:T(8,128)(2,1)} %refs_2_.1, ...), custom_call_target="tpu_custom_call" | custom-call | tf_op jit(solution)/shard_map/pallas_call | solution.py:576
  25.0 3.3 %shard_map.110 = bf16[4,48,32,192]{3,2,1,0:T(8,128)(2,1)} custom-call(bf16[4,26,16,1152]{3,2,1,0:T(8,128)(2,1)S(1)} %get-tuple-element.9.refs_0_, bf16[2,2,256,1536]{3,2,1,0:T(8,128)(2,1)S(1)} %get-tuple-element.10.refs_1_, f32[1,192]{1,0:T(1,128)S(1)} %get-tuple-element.11.refs_2_, f32[2,4,32,32,128]{4,3,2,1,0:T(8,128)S(1)} %get-tuple-element.12.refs_3_), custom_call_target="tpu_custom_call" | custom-call | tf_op jit(solution)/shard_map/pallas_call | solution.py:622

commit v6 on v5

--- a/solution.py
+++ b/solution.py
@@ -33,11 +33,11 @@
     time_bias,
     upsample_weight,
     upsample_bias,
-    taps_2,
-    fold_w,
     offset,
     fine,
     taps_1,
+    taps_2,
+    fold_w,
     wide,
     inner,
     shortcut,
@@ -66,6 +66,7 @@
     corner_f32,
     corner_out,
     corner_in,
+    rows_in,
     load_sem,
     weight_sem,
     send_sem,
@@ -84,6 +85,28 @@
         copy = pltpu.make_async_copy(source, target, sem)
         copy.start()
         return copy
+
+    steps_to = ((-1, 0), (1, 0), (0, -1), (0, 1), (-1, -1), (-1, 1), (1, -1), (1, 1))
+    opposite = (1, 0, 3, 2, 7, 6, 5, 4)
+    has = {
+        (-1, 0): row > 0,
+        (1, 0): row < rows - 1,
+        (0, -1): col > 0,
+        (0, 1): col < cols - 1,
+    }
+    exists = [has[step] if step in has else has[step[0], 0] & has[0, step[1]] for step in steps_to]
+
+    def one(flag):
+        return jnp.where(flag, 1, 0)
+
+    barrier = pltpu.get_barrier_semaphore()
+    for (down, along), there in zip(steps_to, exists) if linked else ():
+
+        @pl.when(there)
+        def _():
+            pl.semaphore_signal(
+                barrier, inc=1, device_id=(row + down, col + along), device_id_type=MESH
+            )
 
     got_inner = load(block_inner, inner, load_sem.at[0])
     got_gain = load(norm_gain, gain, load_sem.at[2])
@@ -104,28 +127,6 @@
             got_up_w = load(upsample_weight, up_w, load_sem.at[3])
     got_shortcut = load(block_input, shortcut, load_sem.at[4])
 
-    steps_to = ((-1, 0), (1, 0), (0, -1), (0, 1), (-1, -1), (-1, 1), (1, -1), (1, 1))
-    opposite = (1, 0, 3, 2, 7, 6, 5, 4)
-    has = {
-        (-1, 0): row > 0,
-        (1, 0): row < rows - 1,
-        (0, -1): col > 0,
-        (0, 1): col < cols - 1,
-    }
-    exists = [has[step] if step in has else has[step[0], 0] & has[0, step[1]] for step in steps_to]
-
-    def one(flag):
-        return jnp.where(flag, 1, 0)
-
-    barrier = pltpu.get_barrier_semaphore()
-    for (down, along), there in zip(steps_to, exists) if linked else ():
-
-        @pl.when(there)
-        def _():
-            pl.semaphore_signal(
-                barrier, inc=1, device_id=(row + down, col + along), device_id_type=MESH
-            )
-
     chunks = channels // LANES
     flat = wide.reshape(chunks, 4 * tall * PITCH, LANES)
 
@@ -181,9 +182,9 @@
         send(turn, 2, source.at[0], target.at[1], sem)
         send(turn, 3, source.at[1], target.at[0], sem + 1)
 
-    def send_rows(turn, taps):
-        send(turn, 0, taps.at[:, 1, :, middle], taps.at[:, tall - 1, :, middle], 0)
-        send(turn, 1, taps.at[:, height, :, middle], taps.at[:, 0, :, middle], 1)
+    def send_rows(turn, taps, targets):
+        send(turn, 0, taps.at[:, 1, :, middle], targets[1], 0)
+        send(turn, 1, taps.at[:, height, :, middle], targets[0], 1)
 
     def send_corners(turn):
         for corner in range(4):
@@ -217,12 +218,17 @@
                         ]
                     done += size
 
-    def place_rows(turn, taps):
-        for end, at in ((0, 0), (1, tall - 1)):
+    ends_of = ((0, 0), (1, tall - 1))
+
+    def place_rows(rows_of):
+        for end, at in ends_of:
             for frame in range(4):
-                values = taps[frame, at, :, middle].astype(F32)
+                values = rows_of(frame, end, at).astype(F32)
                 for k in range(chunks):
                     wide[k, frame * tall + at, BASE : BASE + breadth, :] = values[:, lanes_of(k)]
+
+    def place_corners(turn):
+        for end, at in ends_of:
             for side, place in ((0, BASE - 1), (1, BASE + breadth)):
                 values = corner_in[turn, end * 2 + side].astype(F32)
                 for frame in range(4):
@@ -261,10 +267,12 @@
 
     def send_rows_1():
         pick_corners(corner_out.at[0])
-        send_rows(0, taps_1)
+        send_rows(0, taps_1, [taps_1.at[:, at, :, middle] for at in (0, tall - 1)])
         send_corners(0)
 
     def outside():
+        for at in (0, tall - 1):
+            taps_2[:, at] = jnp.zeros((4, breadth, 3 * channels), BF16)
         got_conv_b.wait()
         conv_b_row[...] = conv_b[...][None, :]
         got_time_b.wait()
@@ -275,8 +283,8 @@
 
             @pl.when(jnp.logical_not(has[end, 0]))
             def _():
-                for taps in (taps_1, taps_2):
-                    taps[:, at, :, middle] = jnp.zeros((4, breadth, channels), BF16)
+                taps_1[:, at, :, middle] = jnp.zeros((4, breadth, channels), BF16)
+                rows_in[at // height] = jnp.zeros((4, breadth, channels), BF16)
 
         for side, along in ((0, -1), (1, 1)):
 
@@ -386,7 +394,8 @@
 
     def rows_1():
         await_from(0, (0, 1, 4, 5, 6, 7))
-        place_rows(0, taps_1)
+        place_rows(lambda frame, end, at: taps_1[frame, at, :, middle])
+        place_corners(0)
         for frame in range(4):
             for at in (0, tall - 1):
                 shift(taps_1, frame, at, 1)
@@ -436,61 +445,65 @@
         time_conv(rim_rows)
 
     def send_rim_2():
-        send_rows(1, taps_2)
+        send_rows(1, taps_2, [rows_in.at[end] for end in range(2)])
         pick_edges(rim_rows, rim_out)
         send_edges(1, rim_out, rim_in, 8)
         pick_corners(corner_out.at[1])
         send_corners(1)
 
-    def up_core():
+    def up_inside():
         for place in (BASE - 1, BASE + breadth):
             for frame in range(4):
-                start = (frame * tall + 1) * PITCH + place
+                start = frame * tall * PITCH + place
                 for k in range(chunks):
-                    flat[k, pl.ds(start, height, stride=PITCH), :] = jnp.zeros((height, LANES), F32)
+                    flat[k, pl.ds(start, tall, stride=PITCH), :] = jnp.zeros((tall, LANES), F32)
         for frame in range(4):
-            shift(taps_2, frame, rim, core + 2)
-        upsample(taps_2, fold_w, rim, core, fine, 0)
+            shift(taps_2, frame, 1, height)
+        upsample(taps_2, fold_w, 0, height, fine, 0)
 
     def receive_2():
         await_from(1, range(10))
         place_columns(core_in, core_rows)
         place_columns(rim_in, rim_rows)
-        flat_fine = fine.reshape(2, 4 * 2 * core * 2 * breadth, LANES)
+        place_rows(lambda frame, end, at: rows_in[end, frame])
+        for end, at in ends_of:
+            for frame in range(4):
+                shift(taps_2, frame, at, 1)
+                taps_2[frame, at, :, middle] = rows_in[end, frame]
+        place_corners(1)
+        flat_fine = fine.reshape(2, 4 * 2 * height * 2 * breadth, LANES)
         for q in range(2):
             place = BASE - 1 + q * (breadth + 1)
+            columns = []
+            for first in range(3):
+                parts = []
+                for frame in range(4):
+                    start = (frame * tall + first) * PITCH + place
+                    spots = pl.ds(start, height, stride=PITCH)
+                    parts.append(jnp.concatenate([flat[k, spots, :] for k in range(chunks)], axis=1))
+                columns.append(jnp.concatenate(parts, axis=0).astype(BF16))
             for p in range(2):
                 summed = 0.0
                 for d in range(2):
-                    first = rim + p + d - 1
-                    x = jnp.concatenate(
-                        [
-                            jnp.concatenate(
-                                [
-                                    flat[k, pl.ds(start, core, stride=PITCH), :]
-                                    for k in range(chunks)
-                                ],
-                                axis=1,
-                            )
-                            for start in [
-                                (frame * tall + 1 + first) * PITCH + place for frame in range(4)
-                            ]
-                        ],
-                        axis=0,
-                    ).astype(BF16)
                     lanes = pl.ds((2 * d + q) * channels, channels)
-                    summed = summed + dot_t(x, fold_w[p, q, :, lanes])
+                    summed = summed + dot_t(columns[p + d], fold_w[p, q, :, lanes])
                 for frame in range(4):
-                    start = (frame * 2 * core + p) * 2 * breadth + q * (2 * breadth - 1)
-                    spots = pl.ds(start, core, stride=4 * breadth)
+                    start = (frame * 2 * height + p) * 2 * breadth + q * (2 * breadth - 1)
+                    spots = pl.ds(start, height, stride=4 * breadth)
                     for k in range(2):
                         flat_fine[k, spots, :] += summed[
-                            frame * core : (frame + 1) * core, lanes_of(k)
+                            frame * height : (frame + 1) * height, lanes_of(k)
                         ]
-        place_rows(1, taps_2)
-        for frame in range(4):
-            shift(taps_2, frame, 0, rim + 2)
-            shift(taps_2, frame, height - rim, rim + 2)
+        for q in range(2):
+            for p, at in ends_of:
+                x = taps_2[:, at, :, q * channels : (q + 2) * channels]
+                w = fold_w[p, q, :, 2 * p * channels : 2 * (p + 1) * channels]
+                summed = dot_t(x.reshape(4 * breadth, 2 * channels), w)
+                for frame in range(4):
+                    for k in range(2):
+                        fine[k, frame, p * (2 * height - 1), pl.ds(q, breadth, stride=2), :] += summed[
+                            frame * breadth : (frame + 1) * breadth, lanes_of(k)
+                        ]
 
     def sent():
         for index, copy in sent_copies:
@@ -498,8 +511,8 @@
 
     steps = (
         begin, send_columns_1, outside, core_middle_pair, send_rows_1, core_middle_ends, time_past,
-        columns_1, core_pair, rows_1, conv_rim, time_rim, send_rim_2, core_ends, time_core,
-        send_core_2, up_core, receive_2, sent,
+        columns_1, core_pair, core_ends, rows_1, conv_rim, time_rim, send_rim_2, time_core,
+        send_core_2, up_inside, receive_2, sent,
     )
     for step in steps:
         step()
@@ -525,30 +538,22 @@
                         ]
 
 
-def upsample_kernel(dims, taps, fold_w, offset, core_fine, out, fine, fine_out, store_sem):
-    height, breadth, channels, up_channels = dims
-    rim = height // 6
-    core = height - 2 * rim
-
-    def store(index, source, start, to, count):
+def store_kernel(parts, offset, fine, out, fine_out, store_sem):
+    up_channels = out.shape[-1]
+    count = out.shape[1] // parts
+    stores = []
+    for part in range(parts):
+        here = pl.ds(part * count, count)
         for k in range(2):
             lanes = slice(k * LANES, min((k + 1) * LANES, up_channels))
             size = lanes.stop - lanes.start
-            values = source[k, :, pl.ds(start, count), :, 0:size]
-            values = values + offset[:, lanes].reshape(1, 1, 1, size)
-            fine_out[:, pl.ds(to, count), :, lanes] = values.astype(BF16)
-        here = pl.ds(to, count)
-        copy = pltpu.make_async_copy(fine_out.at[:, here], out.at[:, here], store_sem.at[index])
-        copy.start()
-        return copy
-
-    stores = [store(0, core_fine, 0, 2 * rim, 2 * core)]
-    for index, first in ((1, 0), (2, height - rim)):
-        to = 2 * rim * (index - 1)
-        upsample(taps, fold_w, first, rim, fine, to)
-        stores.append(store(index, fine, to, 2 * first, 2 * rim))
-    for copy in stores:
-        copy.wait()
+            values = fine[k, :, here, :, 0:size] + offset[:, lanes].reshape(1, 1, 1, size)
+            fine_out[:, here, :, lanes] = values.astype(BF16)
+        store = pltpu.make_async_copy(fine_out.at[:, here], out.at[:, here], store_sem.at[part])
+        store.start()
+        stores.append(store)
+    for store in stores:
+        store.wait()
 
 
 def solution(mesh):
@@ -567,10 +572,8 @@
         field = (rows, cols, height, breadth, channels, up_channels)
         taps_shape = (4, tall, breadth, 3 * channels)
         passed = (
-            vmem(taps_shape, BF16),
-            vmem((2, 2, 2 * LANES, 4 * channels), BF16),
             vmem((1, up_channels), F32),
-            vmem((2, 4, 2 * core, 2 * breadth, LANES), F32),
+            vmem((2, 4, 2 * height, 2 * breadth, LANES), F32),
         )
         whole = pl.BlockSpec(memory_space=pltpu.VMEM)
         passed_on = pl.pallas_call(
@@ -580,6 +583,8 @@
             out_specs=(whole,) * len(passed),
             scratch_shapes=[
                 vmem(taps_shape, BF16),
+                vmem(taps_shape, BF16),
+                vmem((2, 2, 2 * LANES, 4 * channels), BF16),
                 vmem((chunks, 4 * tall, PITCH, LANES), F32),
                 vmem((2, height, breadth, channels), BF16),
                 vmem((2, height, breadth, channels), BF16),
@@ -608,28 +613,26 @@
                 vmem((4, 16, LANES), F32),
                 vmem((2, 4, 16, LANES), BF16),
                 vmem((2, 4, 16, LANES), BF16),
+                vmem((2, 4, breadth, channels), BF16),
                 dma((10,)),
                 dma((3, 3)),
                 dma((2, 10)),
                 dma((2, 10)),
             ],
             compiler_params=pltpu.CompilerParams(
-                collective_id=0, has_side_effects=True, vmem_limit_bytes=40 * 2**20
+                collective_id=0, has_side_effects=True, vmem_limit_bytes=46 * 2**20
             ),
         )(*args)
         passed_on = [pltpu.with_memory_space_constraint(x, pltpu.VMEM) for x in passed_on]
         fine = (4, 2 * height, 2 * breadth)
+        parts = 4
         return pl.pallas_call(
-            lambda *refs: upsample_kernel((height, breadth, channels, up_channels), *refs),
+            lambda *refs: store_kernel(parts, *refs),
             out_shape=jax.ShapeDtypeStruct(fine + (up_channels,), BF16),
             in_specs=[whole] * len(passed),
             out_specs=pl.BlockSpec(memory_space=pl.ANY),
-            scratch_shapes=[
-                vmem((2, 4, 4 * rim, 2 * breadth, LANES), F32),
-                vmem(fine + (up_channels,), BF16),
-                dma((3,)),
-            ],
-            compiler_params=pltpu.CompilerParams(vmem_limit_bytes=32 * 2**20),
+            scratch_shapes=[vmem(fine + (up_channels,), BF16), dma((parts,))],
+            compiler_params=pltpu.CompilerParams(vmem_limit_bytes=16 * 2**20),
         )(*passed_on)
 
     placed = (P(None, "row", "col", None),) * 4 + (P(),) * 7

time: 28.5 us -> 28.2 us (0.989)
  Pallas kernels: 28.3 us -> 27.9 us
    pallas_call x1, Pallas kernels: 3.34 us -> 1.82 us  [on_device(): pl.pallas_call(lambda *refs: store_kernel(parts, *refs), out_shape=jax.Sh...]
    pallas_call x1, Pallas kernels: 24.9 us -> 26.1 us  [on_device(): pl.pallas_call(lambda *refs: field_kernel(field, *refs), out_shape=passed...]
where the time goes in v6:
time: 28.2 us; the launch traced here: 28.1 us
  Pallas kernels  27.9 us (99%)
    pallas_call x1, Pallas kernels, on_device(): pl.pallas_call(lambda *refs: field_kernel(field, *refs), out_shape=passed...  26.1 us
    pallas_call x1, Pallas kernels, on_device(): pl.pallas_call(lambda *refs: store_kernel(parts, *refs), out_shape=jax.Sh...  1.82 us

profile of v6, /device:TPU:107, one launch (start us, length us, event | category | flops | bytes accessed | tf_op | source)
XLA Modules:
  0.0 28.1 jit_solution(7596426708867095386)
XLA Ops:
  0.0 26.1 %shard_map.109 = (f32[1,192]{1,0:T(1,128)S(1)}, f32[2,4,48,32,128]{4,3,2,1,0:T(8,128)S(1)}) custom-call(bf16[2,24,16,384]{3,2,1,0:T(8,128)(2,1)} %refs_0_.1, bf16[2,24,16,384]{3,2,1,0:T(8,128)(2,1)} %refs_1_.1, bf16[2,24,16,384]{3,2,1,0:T(8,128)(2,1)} %refs_2_.1, bf16[2,24,16,384]{3,2,1,0:T(8,128)(2,1)} %refs_3_.1, f32[384]{0:T(512)} %refs_4_.1, ...), custom_call_target="tpu_custom_call" | custom-call | tf_op jit(solution)/shard_map/pallas_call | solution.py:579
  26.1 1.8 %shard_map.110 = bf16[4,48,32,192]{3,2,1,0:T(8,128)(2,1)} custom-call(f32[1,192]{1,0:T(1,128)S(1)} %get-tuple-element.7.refs_0_, f32[2,4,48,32,128]{4,3,2,1,0:T(8,128)S(1)} %get-tuple-element.8.refs_1_), custom_call_target="tpu_custom_call" | custom-call | tf_op jit(solution)/shard_map/pallas_call | solution.py:629

commit v7 on v5

--- a/solution.py
+++ b/solution.py
@@ -85,6 +85,28 @@
         copy.start()
         return copy
 
+    steps_to = ((-1, 0), (1, 0), (0, -1), (0, 1), (-1, -1), (-1, 1), (1, -1), (1, 1))
+    opposite = (1, 0, 3, 2, 7, 6, 5, 4)
+    has = {
+        (-1, 0): row > 0,
+        (1, 0): row < rows - 1,
+        (0, -1): col > 0,
+        (0, 1): col < cols - 1,
+    }
+    exists = [has[step] if step in has else has[step[0], 0] & has[0, step[1]] for step in steps_to]
+
+    def one(flag):
+        return jnp.where(flag, 1, 0)
+
+    barrier = pltpu.get_barrier_semaphore()
+    for (down, along), there in zip(steps_to, exists) if linked else ():
+
+        @pl.when(there)
+        def _():
+            pl.semaphore_signal(
+                barrier, inc=1, device_id=(row + down, col + along), device_id_type=MESH
+            )
+
     got_inner = load(block_inner, inner, load_sem.at[0])
     got_gain = load(norm_gain, gain, load_sem.at[2])
     got_conv_b = load(conv_bias, conv_b, load_sem.at[5])
@@ -104,28 +126,6 @@
             got_up_w = load(upsample_weight, up_w, load_sem.at[3])
     got_shortcut = load(block_input, shortcut, load_sem.at[4])
 
-    steps_to = ((-1, 0), (1, 0), (0, -1), (0, 1), (-1, -1), (-1, 1), (1, -1), (1, 1))
-    opposite = (1, 0, 3, 2, 7, 6, 5, 4)
-    has = {
-        (-1, 0): row > 0,
-        (1, 0): row < rows - 1,
-        (0, -1): col > 0,
-        (0, 1): col < cols - 1,
-    }
-    exists = [has[step] if step in has else has[step[0], 0] & has[0, step[1]] for step in steps_to]
-
-    def one(flag):
-        return jnp.where(flag, 1, 0)
-
-    barrier = pltpu.get_barrier_semaphore()
-    for (down, along), there in zip(steps_to, exists) if linked else ():
-
-        @pl.when(there)
-        def _():
-            pl.semaphore_signal(
-                barrier, inc=1, device_id=(row + down, col + along), device_id_type=MESH
-            )
-
     chunks = channels // LANES
     flat = wide.reshape(chunks, 4 * tall * PITCH, LANES)
 
@@ -456,37 +456,33 @@
         await_from(1, range(10))
         place_columns(core_in, core_rows)
         place_columns(rim_in, rim_rows)
+        beside = {}
         flat_fine = fine.reshape(2, 4 * 2 * core * 2 * breadth, LANES)
         for q in range(2):
             place = BASE - 1 + q * (breadth + 1)
+            columns = []
+            for first in range(rim, rim + 3):
+                parts = []
+                for frame in range(4):
+                    start = (frame * tall + first) * PITCH + place
+                    spots = pl.ds(start, core, stride=PITCH)
+                    parts.append(jnp.concatenate([flat[k, spots, :] for k in range(chunks)], axis=1))
+                columns.append(jnp.concatenate(parts, axis=0).astype(BF16))
             for p in range(2):
-                summed = 0.0
-                for d in range(2):
-                    first = rim + p + d - 1
-                    x = jnp.concatenate(
-                        [
-                            jnp.concatenate(
-                                [
-                                    flat[k, pl.ds(start, core, stride=PITCH), :]
-                                    for k in range(chunks)
-                                ],
-                                axis=1,
-                            )
-                            for start in [
-                                (frame * tall + 1 + first) * PITCH + place for frame in range(4)
-                            ]
-                        ],
-                        axis=0,
-                    ).astype(BF16)
-                    lanes = pl.ds((2 * d + q) * channels, channels)
-                    summed = summed + dot_t(x, fold_w[p, q, :, lanes])
-                for frame in range(4):
-                    start = (frame * 2 * core + p) * 2 * breadth + q * (2 * breadth - 1)
-                    spots = pl.ds(start, core, stride=4 * breadth)
-                    for k in range(2):
-                        flat_fine[k, spots, :] += summed[
-                            frame * core : (frame + 1) * core, lanes_of(k)
-                        ]
+                x = jnp.concatenate(columns[p : p + 2], axis=1)
+                ws = [
+                    fold_w[p, q, :, (2 * d + q) * channels : (2 * d + q + 1) * channels]
+                    for d in range(2)
+                ]
+                beside[p, q] = dot_t(x, jnp.concatenate(ws, axis=1))
+        for (p, q), summed in beside.items():
+            for frame in range(4):
+                start = (frame * 2 * core + p) * 2 * breadth + q * (2 * breadth - 1)
+                spots = pl.ds(start, core, stride=4 * breadth)
+                for k in range(2):
+                    flat_fine[k, spots, :] += summed[
+                        frame * core : (frame + 1) * core, lanes_of(k)
+                    ]
         place_rows(1, taps_2)
         for frame in range(4):
             shift(taps_2, frame, 0, rim + 2)
@@ -498,7 +494,7 @@
 
     steps = (
         begin, send_columns_1, outside, core_middle_pair, send_rows_1, core_middle_ends, time_past,
-        columns_1, core_pair, rows_1, conv_rim, time_rim, send_rim_2, core_ends, time_core,
+        columns_1, core_pair, core_ends, rows_1, conv_rim, time_rim, send_rim_2, time_core,
         send_core_2, up_core, receive_2, sent,
     )
     for step in steps:

time: 28.5 us -> 27.6 us (0.968)
  the two profiles are of different devices: /device:TPU:107 before, /device:TPU:132 now
where the time goes in v7:
time: 27.6 us; the launch traced here: 27.5 us
  Pallas kernels  27.3 us (99%)
    pallas_call x1, Pallas kernels, on_device(): pl.pallas_call(lambda *refs: field_kernel(field, *refs), out_shape=passed...  24 us
    pallas_call x1, Pallas kernels, on_device(): pl.pallas_call(lambda *refs: upsample_kernel((height, breadth, channels,...  3.33 us

profile of v7, /device:TPU:132, one launch (start us, length us, event | category | flops | bytes accessed | tf_op | source)
XLA Modules:
  0.0 27.5 jit_solution(7822551167043880738)
XLA Ops:
  0.0 24.0 %shard_map.109 = (bf16[4,26,16,1152]{3,2,1,0:T(8,128)(2,1)S(1)}, bf16[2,2,256,1536]{3,2,1,0:T(8,128)(2,1)S(1)}, f32[1,192]{1,0:T(1,128)S(1)}, f32[2,4,32,32,128]{4,3,2,1,0:T(8,128)S(1)}) custom-call(bf16[2,24,16,384]{3,2,1,0:T(8,128)(2,1)} %refs_0_.1, bf16[2,24,16,384]{3,2,1,0:T(8,128)(2,1)} %refs_1_.1, bf16[2,24,16,384]{3,2,1,0:T(8,128)(2,1)} %refs_2_.1, ...), custom_call_target="tpu_custom_call" | custom-call | tf_op jit(solution)/shard_map/pallas_call | solution.py:572
  24.0 3.3 %shard_map.110 = bf16[4,48,32,192]{3,2,1,0:T(8,128)(2,1)} custom-call(bf16[4,26,16,1152]{3,2,1,0:T(8,128)(2,1)S(1)} %get-tuple-element.9.refs_0_, bf16[2,2,256,1536]{3,2,1,0:T(8,128)(2,1)S(1)} %get-tuple-element.10.refs_1_, f32[1,192]{1,0:T(1,128)S(1)} %get-tuple-element.11.refs_2_, f32[2,4,32,32,128]{4,3,2,1,0:T(8,128)S(1)} %get-tuple-element.12.refs_3_), custom_call_target="tpu_custom_call" | custom-call | tf_op jit(solution)/shard_map/pallas_call | solution.py:618

commit v8 on v7

--- a/solution.py
+++ b/solution.py
@@ -453,7 +453,7 @@
         upsample(taps_2, fold_w, rim, core, fine, 0)
 
     def receive_2():
-        await_from(1, range(10))
+        await_from(1, (2, 3, 8, 9))
         place_columns(core_in, core_rows)
         place_columns(rim_in, rim_rows)
         beside = {}
@@ -483,6 +483,7 @@
                     flat_fine[k, spots, :] += summed[
                         frame * core : (frame + 1) * core, lanes_of(k)
                     ]
+        await_from(1, (0, 1, 4, 5, 6, 7))
         place_rows(1, taps_2)
         for frame in range(4):
             shift(taps_2, frame, 0, rim + 2)

time: 27.6 us -> 27.1 us (0.982)
  the two profiles are of different devices: /device:TPU:132 before, /device:TPU:107 now
where the time goes in v8:
time: 27.1 us; the launch traced here: 27 us
  Pallas kernels  26.9 us (99%)
    pallas_call x1, Pallas kernels, on_device(): pl.pallas_call(lambda *refs: field_kernel(field, *refs), out_shape=passed...  23.5 us
    pallas_call x1, Pallas kernels, on_device(): pl.pallas_call(lambda *refs: upsample_kernel((height, breadth, channels,...  3.33 us

profile of v8, /device:TPU:107, one launch (start us, length us, event | category | flops | bytes accessed | tf_op | source)
XLA Modules:
  0.0 27.0 jit_solution(6841860747907411903)
XLA Ops:
  0.0 23.5 %shard_map.109 = (bf16[4,26,16,1152]{3,2,1,0:T(8,128)(2,1)S(1)}, bf16[2,2,256,1536]{3,2,1,0:T(8,128)(2,1)S(1)}, f32[1,192]{1,0:T(1,128)S(1)}, f32[2,4,32,32,128]{4,3,2,1,0:T(8,128)S(1)}) custom-call(bf16[2,24,16,384]{3,2,1,0:T(8,128)(2,1)} %refs_0_.1, bf16[2,24,16,384]{3,2,1,0:T(8,128)(2,1)} %refs_1_.1, bf16[2,24,16,384]{3,2,1,0:T(8,128)(2,1)} %refs_2_.1, ...), custom_call_target="tpu_custom_call" | custom-call | tf_op jit(solution)/shard_map/pallas_call | solution.py:573
  23.5 3.3 %shard_map.110 = bf16[4,48,32,192]{3,2,1,0:T(8,128)(2,1)} custom-call(bf16[4,26,16,1152]{3,2,1,0:T(8,128)(2,1)S(1)} %get-tuple-element.9.refs_0_, bf16[2,2,256,1536]{3,2,1,0:T(8,128)(2,1)S(1)} %get-tuple-element.10.refs_1_, f32[1,192]{1,0:T(1,128)S(1)} %get-tuple-element.11.refs_2_, f32[2,4,32,32,128]{4,3,2,1,0:T(8,128)S(1)} %get-tuple-element.12.refs_3_), custom_call_target="tpu_custom_call" | custom-call | tf_op jit(solution)/shard_map/pallas_call | solution.py:619
